TPU v7x, 32 devices: a whole 2x2x4 slice. The times are simulated.
32 devices in a mesh: grid: 8 (over z, x), ch: 4 (over y, core).
Axes of the slice: x: 2, y: 2, z: 4, core: 2. Of those that a mesh axis runs over, the one named last changes fastest.
Arguments:
- inputs: bfloat16 [32, 1024, 512], P('grid', None, 'ch'), may hold values from -6 to 6
- w_gate: bfloat16 [512, 512], P(None, 'ch'), may hold values from -0.25 to 0.25
- w_value: bfloat16 [512, 512], P(None, 'ch'), may hold values from -0.25 to 0.25
- short_filter: bfloat16 [2, 3, 3, 512], P(None, None, None, 'ch'), may hold values from -2 to 2
- row_filter: bfloat16 [1024, 512], P(None, 'ch'), may hold values from -0.1875 to 0.1875
- column_filter: bfloat16 [32, 512], P(None, 'ch'), may hold values from -1 to 1
- cotangent: bfloat16 [32, 1024, 512], P('grid', None, 'ch'), may hold values from -6 to 6
Outputs:
- gated: bfloat16 [32, 1024, 512], P('grid', None, 'ch')
- input_grad: bfloat16 [32, 1024, 512], P('grid', None, 'ch')
- gate_grad: float32 [512, 512], P('grid', 'ch')
- value_grad: float32 [512, 512], P('grid', 'ch')
- short_grad: float32 [2, 3, 3, 512], P(None, None, None, 'ch')
- row_grad: float32 [1024, 512], P('grid', 'ch')
- column_grad: float32 [32, 512], P('grid', 'ch')
All inputs are finite; a program needn't handle non-finite values.
Results may differ from a plain program's by a relative error of at most 0.025.
Values may be sent and summed in bfloat16 or wider, within the bound.
A program may use at most 128 MiB of HBM per device.

v0:
```python
import math

import jax
import jax.numpy as jnp
import ml_dtypes
import numpy as np
from jax import lax
from jax.sharding import PartitionSpec as P

bf16 = jnp.bfloat16
f32 = jnp.float32


def basis(length, tiles):
    half = length // 2
    per = half // tiles
    position = np.arange(length)
    columns, weights = [], []
    for tile in range(tiles):
        freqs = np.arange(tile * per, (tile + 1) * per)
        phase = (position[:, None] * freqs[None, :] % length) * (2.0 * math.pi / length)
        sines = np.sin(phase)
        weight = np.full((2 * per,), 2.0 / length)
        if tile == 0:
            sines[:, 0] = np.where(position % 2 == 0, 1.0, -1.0)
            weight[0] = weight[per] = 1.0 / length
        columns += [np.cos(phase), sines]
        weights.append(weight)
    return np.concatenate(columns, axis=1), np.concatenate(weights)


def parts(spectrum, axis):
    return jnp.split(spectrum, 2, axis=axis)


def filter_parts(spectrum, first):
    cos, sin = parts(spectrum, 0)
    row = lax.broadcasted_iota(jnp.int32, cos.shape, 0) == 0
    packed = jnp.logical_and(row, first)
    return cos, jnp.where(packed, 0.0, sin), jnp.where(packed, sin, cos)


def times(spectrum, coef, axis):
    x, y = parts(spectrum, axis)
    p, q, p2 = coef
    return jnp.concatenate([x * p - y * q, x * q + y * p2], axis=axis)


def times_conj(spectrum, coef, axis):
    x, y = parts(spectrum, axis)
    p, q, p2 = coef
    return jnp.concatenate([x * p + y * q, y * p2 - x * q], axis=axis)


def correlate(a, b, axis, total, first):
    ax, ay = parts(a, axis)
    bx, by = parts(b, axis)
    xx, yy = jnp.sum(ax * bx, axis=total), jnp.sum(ay * by, axis=total)
    cross = jnp.sum(ay * bx - ax * by, axis=total)
    row = lax.broadcasted_iota(jnp.int32, xx.shape, 0) == 0
    packed = jnp.logical_and(row, first)
    return jnp.concatenate(
        [jnp.where(packed, xx, xx + yy), jnp.where(packed, yy, cross)], axis=0
    )


def dot(spec, a, b):
    return jnp.einsum(spec, a.astype(bf16), b.astype(bf16), preferred_element_type=f32)


def neighbours(last, initial):
    size = lax.axis_size("grid")
    before = lax.ppermute(last, "grid", [(i, i + 1) for i in range(size - 1)])
    after = lax.ppermute(initial, "grid", [(i + 1, i) for i in range(size - 1)])
    return before, after


def stencil(rows, kernel, flipped):
    width = rows[0].shape[1]
    framed = jnp.pad(jnp.concatenate(rows, axis=0), ((0, 0), (1, 1), (0, 0)))
    count = len(rows) - 2
    total = jnp.zeros((count, width, rows[0].shape[2]), f32)
    for i in range(3):
        for j in range(3):
            weight = kernel[2 - i, 2 - j] if flipped else kernel[i, j]
            total = total + weight * framed[i : i + count, j : j + width].astype(f32)
    return total.astype(bf16), framed


def split_rows(value):
    return [value[i : i + 1] for i in range(value.shape[0])]


def filter_sums(grad, framed):
    rows, width, _ = grad.shape
    grad = grad.astype(f32)
    return [
        jnp.sum(grad * framed[i : i + rows, j : j + width].astype(f32), axis=(0, 1))
        for i in range(3)
        for j in range(3)
    ]


def gather(value):
    size = lax.axis_size("ch")
    swap = [(i, i ^ 1) for i in range(size)]
    held = [value] + [
        lax.ppermute(value, "ch", [(i, (i - 2 * hop) % size) for i in range(size)])
        for hop in range(1, size // 2)
    ]
    blocks = []
    for block in held:
        blocks += [block, lax.ppermute(block, "ch", swap)]
    return jnp.concatenate(blocks, axis=2)


def scatter_sum(value, mates, others):
    size = lax.axis_size("ch")
    chips = size // 2
    channels = others.shape[1] // chips
    sent = dot("rwc,cd->rwd", value, mates).astype(bf16)
    got = lax.ppermute(sent, "ch", [(i, i ^ 1) for i in range(size)])
    pair = dot("rwc,cd->rwd", value, others) + got.astype(f32)
    total = pair[..., :channels]
    for hop in range(1, chips):
        part = pair[..., hop * channels : (hop + 1) * channels].astype(bf16)
        total = total + lax.ppermute(
            part, "ch", [(i, (i + 2 * hop) % size) for i in range(size)]
        ).astype(f32)
    return total.astype(bf16)


def local(inputs, w_gate, w_value, short_filter, row_filter, column_filter, cotangent):
    tile_rows, width, channels = inputs.shape
    height = column_filter.shape[0]
    tiles = lax.axis_size("grid")
    me = lax.axis_index("grid")
    first = me == 0
    per = width // tiles
    scale = 1.0 / math.sqrt(height * width)
    chips = lax.axis_size("ch") // 2
    spot = lax.axis_index("ch")

    edges = jnp.concatenate([inputs[:1], inputs[-1:]], axis=0)
    edges = gather(edges)
    middle = gather(inputs[1:-1])
    w_both = jnp.concatenate([w_gate, w_value], axis=1)

    wide, wide_weight = basis(width, tiles)
    tall, tall_weight = basis(height, 1)
    wide = jnp.asarray(wide.astype(ml_dtypes.bfloat16))
    tall = jnp.asarray(tall.astype(ml_dtypes.bfloat16))
    tall_weight = jnp.asarray(tall_weight, f32)[:, None]
    wide_weight = lax.dynamic_slice_in_dim(jnp.asarray(wide_weight, f32), me * per, per, 0)[:, None]
    wide_own = lax.dynamic_slice_in_dim(wide, me * per, per, 1)
    kernel = short_filter.astype(f32)
    row_coef = filter_parts(dot("mk,mc->kc", wide_own, row_filter), first)
    col_coef = filter_parts(dot("mk,mc->kc", tall, column_filter), True)
    col_coef = tuple(v[:, None, :] for v in col_coef)

    def block(hop, swap):
        index = (spot // 2 + hop) % chips * 2 + (spot % 2 + swap) % 2
        return lax.dynamic_slice_in_dim(w_both, index * channels, channels, 0)

    blocks = [[block(hop, swap) for swap in range(2)] for hop in range(chips)]
    mates = jnp.concatenate([pair[1].T for pair in blocks], axis=1)
    others = jnp.concatenate([pair[0].T for pair in blocks], axis=1)
    w_turned = jnp.concatenate([both for pair in blocks for both in pair], axis=0)

    def unturned(term):
        pieces = []
        for chip in range(chips):
            for core in range(2):
                place = (chip - spot // 2) % chips * 2 + (core - spot % 2) % 2
                pieces.append(lax.dynamic_slice_in_dim(term, place * channels, channels, 0))
        return jnp.concatenate(pieces, axis=0)

    edge_proj = dot("rwd,dc->rwc", edges, w_turned).astype(bf16)
    edge_b, edge_a = edge_proj[..., channels:], edge_proj[..., :channels]
    before_b, after_b = neighbours(edge_b[1:], edge_b[:1])
    before_a, after_a = neighbours(edge_a[1:], edge_a[:1])
    mid_proj = dot("rwd,dc->rwc", middle, w_turned).astype(bf16)
    mid_b, mid_a = mid_proj[..., channels:], mid_proj[..., :channels]
    value_bf, framed_b = stencil(
        [before_b, edge_b[:1], *split_rows(mid_b), edge_b[1:], after_b], kernel[1], False
    )

    def spectrum_of(field):
        return dot("wk,rwc->rkc", wide, field).astype(bf16)

    def to_columns(spectrum):
        return lax.all_to_all(spectrum, "grid", split_axis=1, concat_axis=0, tiled=True).astype(f32)

    def to_rows(spectrum):
        spectrum = (spectrum * wide_weight).astype(bf16)
        back = lax.all_to_all(spectrum, "grid", split_axis=0, concat_axis=1, tiled=True)
        return dot("wk,rkc->rwc", wide, back)

    value_rows, before_a, after_a = lax.optimization_barrier(
        (spectrum_of(value_bf), before_a, after_a)
    )
    value_spec = to_columns(value_rows)
    gate_bf, framed_a = stencil(
        [before_a, edge_a[:1], *split_rows(mid_a), edge_a[1:], after_a], kernel[0], False
    )
    gate_feat = gate_bf.astype(f32)
    grad_out = cotangent.astype(f32)
    grad_mix = (grad_out * gate_feat).astype(bf16)
    grad_rows, value_spec = lax.optimization_barrier((spectrum_of(grad_mix), value_spec))
    grad_spec = to_columns(grad_rows)

    mixed_rows = times(value_spec, row_coef, 1)
    value_tall = dot("hk,hwc->kwc", tall, mixed_rows)
    mixed = dot("hk,kwc->hwc", tall, times(value_tall, col_coef, 0) * tall_weight[:, None])
    mix_col = to_rows(mixed)

    grad_tall = dot("hk,hwc->kwc", tall, grad_spec)
    grad_row = dot("hk,kwc->hwc", tall, times_conj(grad_tall, col_coef, 0) * tall_weight[:, None])
    grad_value = to_rows(times_conj(grad_row, row_coef, 1)).astype(bf16)

    col_term = correlate(grad_tall * wide_weight, value_tall, 0, 1, True)
    col_grad = dot("mk,kc->mc", tall, col_term * tall_weight) * scale
    row_term = correlate(grad_row, value_spec, 1, 0, first)
    row_grad = dot("mk,kc->mc", wide_own, row_term * wide_weight) * scale

    gated = (gate_feat * mix_col).astype(bf16)
    grad_gate = (grad_out * mix_col).astype(bf16)

    def back_parts(grad, filt):
        before, after = neighbours(grad[-1:], grad[:1])
        rows = split_rows(grad)
        middle_back, _ = stencil(rows, filt, True)
        top, _ = stencil([before, rows[0], rows[1]], filt, True)
        bottom, _ = stencil([rows[-2], rows[-1], after], filt, True)
        return middle_back, jnp.concatenate([top, bottom], axis=0)

    mid_back_a, edge_back_a = back_parts(grad_gate, kernel[0])
    mid_back_b, edge_back_b = back_parts(grad_value, kernel[1])
    mid_back = jnp.concatenate([mid_back_a, mid_back_b], axis=2)
    edge_back = jnp.concatenate([edge_back_a, edge_back_b], axis=2)
    mid_grad = scatter_sum(mid_back, mates, others)
    edge_grad = scatter_sum(edge_back, mates, others)
    input_grad = jnp.concatenate([edge_grad[:1], mid_grad, edge_grad[1:]], axis=0)

    gate_term = dot("rwd,rwc->dc", middle, mid_back_a) + dot("rwd,rwc->dc", edges, edge_back_a)
    value_term = dot("rwd,rwc->dc", middle, mid_back_b) + dot("rwd,rwc->dc", edges, edge_back_b)
    short_term = jnp.stack(filter_sums(grad_gate, framed_a) + filter_sums(grad_value, framed_b))
    short_term = short_term * scale
    depth = w_both.shape[0]

    def cut(term):
        return term.reshape(tiles, term.shape[0] // tiles, channels)

    packed = jnp.concatenate(
        [
            cut(unturned(gate_term * scale)),
            cut(unturned(value_term * scale)),
            cut(row_grad),
            cut(col_grad),
            jnp.broadcast_to(short_term[None], (tiles, 18, channels)),
        ],
        axis=1,
    ).astype(bf16)
    arrived = lax.all_to_all(packed, "grid", split_axis=0, concat_axis=0, tiled=True)
    total = jnp.sum(arrived.astype(f32), axis=0)
    ends = np.cumsum([depth // tiles, depth // tiles, per, height // tiles])
    gate_grad, value_grad, row_share, col_share, short_sum = jnp.split(total, ends, axis=0)
    return (
        gated,
        input_grad,
        gate_grad,
        value_grad,
        short_sum.reshape(2, 3, 3, channels),
        row_share,
        col_share,
    )


def solution(mesh):
    return jax.shard_map(
        local,
        mesh=mesh,
        in_specs=(
            P("grid", None, "ch"),
            P(None, "ch"),
            P(None, "ch"),
            P(None, None, None, "ch"),
            P(None, "ch"),
            P(None, "ch"),
            P("grid", None, "ch"),
        ),
        out_specs=(
            P("grid", None, "ch"),
            P("grid", None, "ch"),
            P("grid", "ch"),
            P("grid", "ch"),
            P(None, None, None, "ch"),
            P("grid", "ch"),
            P("grid", "ch"),
        ),
        check_vma=False,
    )
```

profile of v0, /device:TPU:0, one launch (start us, length us, event | category | flops | bytes accessed | tf_op | source)
XLA Modules:
  0.0 290.2 jit_solution(11565719158127112747)
XLA Ops:
  1.9 3.0 %collective-permute-start.1 = (bf16[2,1024,128]{2,1,0:T(8,128)(2,1)S(1)}, bf16[2,1024,128]{2,1,0:T(8,128)(2,1)S(1)}, u32[]{:S(2)}, u32[]{:S(2)}) collective-permute-start(bf16[2,1024,128]{2,1,0:T(8,128)(2,1)S(1)} %pad_maximum_fusion.14), channel_id=1, source_target_pairs={{0,2},{1,3},{2,0},{3,1},{4,6},{5,7},{6,4},{7,5},{8,10},{9,11},{10,... | collective-permute-start | bytes 1572872 | tf_op jit(solution)/shard_map/ppermute | solution.py:108
  5.7 12.0 %collective-permute-done.1 = bf16[2,1024,128]{2,1,0:T(8,128)(2,1)S(1)} collective-permute-done((bf16[2,1024,128]{2,1,0:T(8,128)(2,1)S(1)}, bf16[2,1024,128]{2,1,0:T(8,128)(2,1)S(1)}, u32[]{:S(2)}, u32[]{:S(2)}) %collective-permute-start.1) | collective-permute-done | bytes 524320 | tf_op jit(solution)/shard_map/ppermute | solution.py:108
  17.9 10.2 %collective-permute-done.5 = bf16[2,1024,128]{2,1,0:T(8,128)(2,1)S(1)} collective-permute-done((bf16[2,1024,128]{2,1,0:T(8,128)(2,1)S(1)}, bf16[2,1024,128]{2,1,0:T(8,128)(2,1)S(1)}, u32[]{:S(2)}, u32[]{:S(2)}) %collective-permute-start.5) | collective-permute-done | bytes 524320 | tf_op jit(solution)/shard_map/ppermute | solution.py:108
  28.2 2.1 convolution_convert_fusion.1
  30.4 3.6 %collective-permute-start.3 = (bf16[1,1024,128]{2,1,0:T(8,128)(2,1)S(1)}, bf16[1,1024,128]{2,1,0:T(8,128)(2,1)S(1)}, u32[]{:S(2)}, u32[]{:S(2)}) collective-permute-start(bf16[1,1024,128]{2,1,0:T(8,128)(2,1)S(1)} %slice.562), channel_id=1, source_target_pairs={{0,4},{4,8},{8,12},{12,16},{16,20},{20,24},{24,28},{1,5},{5,9},{9,... | collective-permute-start | bytes 786440 | tf_op jit(solution)/shard_map/ppermute | solution.py:73
  34.1 2.1 convolution_convert_fusion
  36.2 3.8 %collective-permute-done.3 = bf16[1,1024,128]{2,1,0:T(8,128)(2,1)S(1)} collective-permute-done((bf16[1,1024,128]{2,1,0:T(8,128)(2,1)S(1)}, bf16[1,1024,128]{2,1,0:T(8,128)(2,1)S(1)}, u32[]{:S(2)}, u32[]{:S(2)}) %collective-permute-start.3) | collective-permute-done | bytes 262176 | tf_op jit(solution)/shard_map/ppermute | solution.py:73
  42.8 5.0 %collective-permute-start.8 = (bf16[1,1024,128]{2,1,0:T(8,128)(2,1)S(1)}, bf16[1,1024,128]{2,1,0:T(8,128)(2,1)S(1)}, u32[]{:S(2)}, u32[]{:S(2)}) collective-permute-start(bf16[1,1024,128]{2,1,0:T(8,128)(2,1)S(1)} %get-tuple-element.90), channel_id=1, source_target_pairs={{0,4},{4,8},{8,12},{12,16},{16,20},{20,24},{24,28},{1,5},{5,9},{9,... | collective-permute-start | bytes 786440 | tf_op jit(solution)/shard_map/ppermute | solution.py:73
  49.1 2.6 collective-permute-done.7
  51.8 6.2 %fusion.43 = bf16[4,1024,128]{1,2,0:T(8,128)(2,1)} fusion(bf16[1024,1024,1]{1,0,2:T(8,128)(2,1)S(1)} %copy-done.6, f32[128]{0:T(128)S(1)} %get-tuple-element.121, f32[128]{0:T(128)S(1)} %get-tuple-element.122, f32[128]{0:T(128)S(1)} %get-tuple-element.123, f32[128]{0:T(128)S(1)} %get-tuple-element.124, f32[128]{0:T(128)S(1)} %get-tuple-element.125, ...), kind=kOutput, calls=%fused_computation.99 | convolution fusion | flops 1096286208 | bytes 6296064 | tf_op jit(solution)/shard_map/wk,rwc->rkc/dot_general | solution.py:68
  58.1 5.0 %collective-permute-done.8 = bf16[1,1024,128]{2,1,0:T(8,128)(2,1)S(1)} collective-permute-done((bf16[1,1024,128]{2,1,0:T(8,128)(2,1)S(1)}, bf16[1,1024,128]{2,1,0:T(8,128)(2,1)S(1)}, u32[]{:S(2)}, u32[]{:S(2)}) %collective-permute-start.8) | collective-permute-done | bytes 262176 | tf_op jit(solution)/shard_map/ppermute | solution.py:73
  63.1 2.6 copy.57
  65.7 8.2 %all-to-all-start = ((bf16[4,1024,128]{2,0,1:T(4,128)(2,1)}), bf16[4,1024,128]{2,0,1:T(4,128)(2,1)S(1)}, u32[]{:S(2)}, u32[]{:S(2)}) async-start(bf16[4,1024,128]{2,0,1:T(4,128)(2,1)} %copy.57), calls=%async_computation | async-start | bytes 2097152 | tf_op jit(solution)/shard_map/all_to_all | solution.py:192
  75.3 3.3 %fusion.17 = bf16[4,1024,128]{2,1,0:T(8,128)(2,1)S(1)} fusion(f32[128]{0:T(128)S(1)} %get-tuple-element.130, f32[128]{0:T(128)S(1)} %get-tuple-element.131, f32[128]{0:T(128)S(1)} %get-tuple-element.132, f32[128]{0:T(128)S(1)} %get-tuple-element.133, f32[128]{0:T(128)S(1)} %get-tuple-element.134, f32[128]{0:T(128)S(1)} %get-tuple-element.135, ...), kind=kLoop, calls=%fused_computation.58 | loop fusion | flops 22020096 | bytes 4198912 | tf_op jit(solution)/shard_map/convert_element_type | solution.py:87
  78.7 2.3 fusion.44
  81.0 16.7 %all-to-all-done = bf16[4,1024,128]{2,0,1:T(4,128)(2,1)S(1)} async-done(((bf16[4,1024,128]{2,0,1:T(4,128)(2,1)}), bf16[4,1024,128]{2,0,1:T(4,128)(2,1)S(1)}, u32[]{:S(2)}, u32[]{:S(2)}) %all-to-all-start) | async-done | bytes 1048608 | tf_op jit(solution)/shard_map/all_to_all | solution.py:192
  98.6 1.8 copy.58
  100.4 2.4 copy.63
  102.8 4.6 %all-to-all-start.2 = ((bf16[4,1024,128]{2,0,1:T(4,128)(2,1)}), bf16[4,1024,128]{2,0,1:T(4,128)(2,1)}, u32[]{:S(2)}, u32[]{:S(2)}) async-start(bf16[4,1024,128]{2,0,1:T(4,128)(2,1)} %copy.63), calls=%async_computation.2 | async-start | bytes 2097152 | tf_op jit(solution)/shard_map/all_to_all | solution.py:192
  110.7 21.2 %all-to-all-done.2 = bf16[4,1024,128]{2,0,1:T(4,128)(2,1)} async-done(((bf16[4,1024,128]{2,0,1:T(4,128)(2,1)}), bf16[4,1024,128]{2,0,1:T(4,128)(2,1)}, u32[]{:S(2)}, u32[]{:S(2)}) %all-to-all-start.2) | async-done | bytes 1048608 | tf_op jit(solution)/shard_map/all_to_all | solution.py:192
  135.2 2.0 multiply_reduce_fusion.3
  138.9 4.3 %all-to-all-start.3 = ((bf16[32,128,128]{2,1,0:T(8,128)(2,1)}), bf16[32,128,128]{2,1,0:T(8,128)(2,1)}, u32[]{:S(2)}, u32[]{:S(2)}) async-start(bf16[32,128,128]{2,1,0:T(8,128)(2,1)} %copy.67), calls=%async_computation.3 | async-start | bytes 2097152 | tf_op jit(solution)/shard_map/all_to_all | solution.py:196
  143.3 1.6 fusion.59
  147.5 2.0 fusion.47
  149.4 19.2 %all-to-all-done.3 = bf16[32,128,128]{2,1,0:T(8,128)(2,1)} async-done(((bf16[32,128,128]{2,1,0:T(8,128)(2,1)}), bf16[32,128,128]{2,1,0:T(8,128)(2,1)}, u32[]{:S(2)}, u32[]{:S(2)}) %all-to-all-start.3) | async-done | bytes 1048608 | tf_op jit(solution)/shard_map/all_to_all | solution.py:196
  168.6 3.8 %all-to-all-start.1 = ((bf16[32,128,128]{2,1,0:T(8,128)(2,1)}), bf16[32,128,128]{2,1,0:T(8,128)(2,1)S(1)}, u32[]{:S(2)}, u32[]{:S(2)}) async-start(bf16[32,128,128]{2,1,0:T(8,128)(2,1)} %copy.60), calls=%async_computation.1 | async-start | bytes 2097152 | tf_op jit(solution)/shard_map/all_to_all | solution.py:196
  173.2 1.7 copy.68
  176.2 9.7 %fusion.38 = (f32[128]{0:T(128)}, f32[128]{0:T(128)}, f32[128]{0:T(128)}, f32[128]{0:T(128)}, f32[128]{0:T(128)}, /*index=5*/f32[128]{0:T(128)}, f32[128]{0:T(12...) fusion(bf16[6,1024,128]{2,1,0:T(8,128)(2,1)} %copy-done.55, bf16[2,1024,128]{2,1,0:T(8,128)(2,1)} %copy-done.27, ...), kind=kOutput, calls=%fused_computation.79 | convolution fusion | flops 1096809344 | bytes 7344640 | tf_op jit(solution)/shard_map/wk,rkc->rwc/dot_general | solution.py:68
  187.9 1.8 add_convert_fusion
  189.7 8.3 %all-to-all-done.1 = bf16[32,128,128]{2,1,0:T(8,128)(2,1)S(1)} async-done(((bf16[32,128,128]{2,1,0:T(8,128)(2,1)}), bf16[32,128,128]{2,1,0:T(8,128)(2,1)S(1)}, u32[]{:S(2)}, u32[]{:S(2)}) %all-to-all-start.1) | async-done | bytes 1048608 | tf_op jit(solution)/shard_map/all_to_all | solution.py:196
  199.5 2.3 all_to_all.53
  201.8 11.6 %fusion.29 = (f32[128]{0:T(128)}, f32[128]{0:T(128)}, f32[128]{0:T(128)}, f32[128]{0:T(128)}, f32[128]{0:T(128)}, /*index=5*/f32[128]{0:T(128)}, f32[128]{0:T(12...) fusion(bf16[6,1024,128]{2,1,0:T(8,128)(2,1)} %copy-done.4, ...), kind=kOutput, calls=%fused_computation.70 | convolution fusion | flops 1099430784 | bytes 10490368 | tf_op jit(solution)/shard_map/wk,rkc->rwc/dot_general | solution.py:68
  215.7 3.2 %collective-permute-start.12 = (bf16[1,1024,128]{2,1,0:T(8,128)(2,1)}, bf16[1,1024,128]{2,1,0:T(8,128)(2,1)S(1)}, u32[]{:S(2)}, u32[]{:S(2)}) collective-permute-start(bf16[1,1024,128]{2,1,0:T(8,128)(2,1)} %get-tuple-element.83), channel_id=1, source_target_pairs={{0,4},{4,8},{8,12},{12,16},{16,20},{20,24},{24,28},{1,5},{5,9},{9,... | collective-permute-start | bytes 786440 | tf_op jit(solution)/shard_map/ppermute | solution.py:73
  220.2 4.6 %collective-permute-start.10 = (bf16[1,1024,128]{2,1,0:T(8,128)(2,1)}, bf16[1,1024,128]{2,1,0:T(8,128)(2,1)S(1)}, u32[]{:S(2)}, u32[]{:S(2)}) collective-permute-start(bf16[1,1024,128]{2,1,0:T(8,128)(2,1)} %get-tuple-element.79), channel_id=1, source_target_pairs={{0,4},{4,8},{8,12},{12,16},{16,20},{20,24},{24,28},{1,5},{5,9},{9,... | collective-permute-start | bytes 786440 | tf_op jit(solution)/shard_map/ppermute | solution.py:73
  224.7 1.6 collective-permute-start.11
  226.3 2.4 convolution_convert_fusion.2
  228.8 8.4 %collective-permute-done.12 = bf16[1,1024,128]{2,1,0:T(8,128)(2,1)S(1)} collective-permute-done((bf16[1,1024,128]{2,1,0:T(8,128)(2,1)}, bf16[1,1024,128]{2,1,0:T(8,128)(2,1)S(1)}, u32[]{:S(2)}, u32[]{:S(2)}) %collective-permute-start.12) | collective-permute-done | bytes 262176 | tf_op jit(solution)/shard_map/ppermute | solution.py:73
  238.4 2.4 collective-permute-done.10
  244.8 1.8 convolution_bitcast_fusion
  246.6 1.9 convolution_bitcast_fusion.2
  248.6 1.8 fusion.51
  250.4 1.8 fusion.49
  252.4 4.2 %concatenate.149 = bf16[8,278,128]{2,1,0:T(8,128)(2,1)} concatenate(bf16[8,64,128]{2,1,0:T(8,128)(2,1)S(1)} %bitcast.157, bf16[8,64,128]{2,1,0:T(8,128)(2,1)S(1)} %bitcast.156, bf16[8,128,128]{2,1,0:T(8,128)(2,1)S(1)} %bitcast.155, bf16[8,4,128]{2,1,0:T(4,128)(2,1)S(1)} %bitcast.166, bf16[8,18,128]{2,1,0:T(8,128)(2,1)S(1)} %broadcast_in_dim.12), dimensions={1} | concatenate | bytes 1138688 | tf_op jit(solution)/shard_map/concatenate | solution.py:254
  256.6 3.7 %all-to-all-start.4 = ((bf16[8,278,128]{2,1,0:T(8,128)(2,1)}), bf16[8,278,128]{2,1,0:T(8,128)(2,1)S(1)}, u32[]{:S(2)}, u32[]{:S(2)}) async-start(bf16[8,278,128]{2,1,0:T(8,128)(2,1)} %concatenate.149), calls=%async_computation.4 | async-start | bytes 1146880 | tf_op jit(solution)/shard_map/all_to_all | solution.py:264
  260.4 2.0 convert_add_fusion
  264.0 1.7 convert_add_fusion.1
  267.7 8.7 %all-to-all-done.4 = bf16[8,278,128]{2,1,0:T(8,128)(2,1)S(1)} async-done(((bf16[8,278,128]{2,1,0:T(8,128)(2,1)}), bf16[8,278,128]{2,1,0:T(8,128)(2,1)S(1)}, u32[]{:S(2)}, u32[]{:S(2)}) %all-to-all-start.4) | async-done | bytes 569376 | tf_op jit(solution)/shard_map/all_to_all | solution.py:264
  280.1 7.7 %collective-permute-done.15 = bf16[2,1024,128]{2,1,0:T(8,128)(2,1)} collective-permute-done((bf16[2,1024,128]{2,1,0:T(8,128)(2,1)}, bf16[2,1024,128]{2,1,0:T(8,128)(2,1)}, u32[]{:S(2)}, u32[]{:S(2)}) %collective-permute-start.15) | collective-permute-done | bytes 524320 | tf_op jit(solution)/shard_map/ppermute | solution.py:127
  (328 shorter events, 43.0 us)
Async XLA Ops:
  0.6 108.7 %copy-start = (bf16[1024,128]{1,0:T(8,128)(2,1)S(1)}, bf16[1024,128]{1,0:T(8,128)(2,1)}, u32[]{:S(2)}) copy-start(bf16[1024,128]{1,0:T(8,128)(2,1)} %param.15) | copy-start | bytes 786436
  0.7 17.1 %copy-start.46 = (bf16[512,128]{1,0:T(8,128)(2,1)S(1)}, bf16[512,128]{1,0:T(8,128)(2,1)}, u32[]{:S(2)}) copy-start(bf16[512,128]{1,0:T(8,128)(2,1)} %param.12) | copy-start | bytes 393220
  0.7 17.1 %copy-start.47 = (bf16[512,128]{1,0:T(8,128)(2,1)S(1)}, bf16[512,128]{1,0:T(8,128)(2,1)}, u32[]{:S(2)}) copy-start(bf16[512,128]{1,0:T(8,128)(2,1)} %param.13) | copy-start | bytes 393220
  0.7 17.2 %copy-start.56 = (bf16[2,3,3,128]{3,0,2,1:T(2,128)(2,1)S(1)}, bf16[2,3,3,128]{3,0,2,1:T(2,128)(2,1)}, u32[]{:S(2)}) copy-start(bf16[2,3,3,128]{3,0,2,1:T(2,128)(2,1)} %param.14) | copy-start | bytes 13828
  1.9 28.4 %copy-start.19 = (bf16[1,1024,128]{2,1,0:T(8,128)(2,1)}, bf16[1,1024,128]{2,1,0:T(8,128)(2,1)S(1)}, u32[]{:S(2)}) copy-start(bf16[1,1024,128]{2,1,0:T(8,128)(2,1)S(1)} %get-tuple-element.92) | copy-start | bytes 786436
  1.9 28.4 %copy-start.21 = (bf16[1,1024,128]{2,1,0:T(8,128)(2,1)}, bf16[1,1024,128]{2,1,0:T(8,128)(2,1)S(1)}, u32[]{:S(2)}) copy-start(bf16[1,1024,128]{2,1,0:T(8,128)(2,1)S(1)} %get-tuple-element.93) | copy-start | bytes 786436
  1.9 15.8 %collective-permute-start.1 = (bf16[2,1024,128]{2,1,0:T(8,128)(2,1)S(1)}, bf16[2,1024,128]{2,1,0:T(8,128)(2,1)S(1)}, u32[]{:S(2)}, u32[]{:S(2)}) collective-permute-start(bf16[2,1024,128]{2,1,0:T(8,128)(2,1)S(1)} %pad_maximum_fusion.14), channel_id=1, source_target_pairs={{0,2},{1,3},{2,0},{3,1},{4,6},{5,7},{6,4},{7,5},{8,10},{9,11},{10,... | collective-permute-start | bytes 1572872 | tf_op jit(solution)/shard_map/ppermute | solution.py:108
  5.0 23.2 %collective-permute-start = (bf16[2,1024,128]{2,1,0:T(8,128)(2,1)S(1)}, bf16[2,1024,128]{2,1,0:T(8,128)(2,1)}, u32[]{:S(2)}, u32[]{:S(2)}) collective-permute-start(bf16[2,1024,128]{2,1,0:T(8,128)(2,1)S(1)} %pad_maximum_fusion.14), channel_id=1, source_target_pairs={{0,1},{1,0},{2,3},{3,2},{4,5},{5,4},{6,7},{7,6},{8,9},{9,8},{10,11... | collective-permute-start | bytes 1572872 | tf_op jit(solution)/shard_map/ppermute | solution.py:113
  5.0 29.0 %copy-start.28 = (bf16[2,1024,128]{2,1,0:T(8,128)(2,1)}, bf16[2,1024,128]{2,1,0:T(8,128)(2,1)S(1)}, u32[]{:S(2)}) copy-start(bf16[2,1024,128]{2,1,0:T(8,128)(2,1)S(1)} %slice.469) | copy-start | bytes 1572868
  5.0 23.1 %collective-permute-start.5 = (bf16[2,1024,128]{2,1,0:T(8,128)(2,1)S(1)}, bf16[2,1024,128]{2,1,0:T(8,128)(2,1)S(1)}, u32[]{:S(2)}, u32[]{:S(2)}) collective-permute-start(bf16[2,1024,128]{2,1,0:T(8,128)(2,1)S(1)} %slice.469), channel_id=1, source_target_pairs={{0,2},{1,3},{2,0},{3,1},{4,6},{5,7},{6,4},{7,5},{8,10},{9,11},{10,... | collective-permute-start | bytes 1572872 | tf_op jit(solution)/shard_map/ppermute | solution.py:108
  5.2 28.8 %collective-permute-start.4 = (bf16[2,1024,128]{2,1,0:T(8,128)(2,1)S(1)}, bf16[2,1024,128]{2,1,0:T(8,128)(2,1)}, u32[]{:S(2)}, u32[]{:S(2)}) collective-permute-start(bf16[2,1024,128]{2,1,0:T(8,128)(2,1)S(1)} %slice.469), channel_id=1, source_target_pairs={{0,1},{1,0},{2,3},{3,2},{4,5},{5,4},{6,7},{7,6},{8,9},{9,8},{10,11... | collective-permute-start | bytes 1572872 | tf_op jit(solution)/shard_map/ppermute | solution.py:113
  17.7 10.4 %collective-permute-start.2 = (bf16[2,1024,128]{2,1,0:T(8,128)(2,1)S(1)}, bf16[2,1024,128]{2,1,0:T(8,128)(2,1)S(1)}, u32[]{:S(2)}, u32[]{:S(2)}) collective-permute-start(bf16[2,1024,128]{2,1,0:T(8,128)(2,1)S(1)} %collective-permute-done.1), channel_id=1, source_target_pairs={{0,1},{1,0},{2,3},{3,2},{4,5},{5,4},{6,7},{7,6},{8,9},{9,8},{10,11... | collective-permute-start | bytes 1572872 | tf_op jit(solution)/shard_map/ppermute | solution.py:113
  17.9 16.2 %copy-start.49 = (bf16[128,256]{1,0:T(8,128)(2,1)}, bf16[128,256]{1,0:T(8,128)(2,1)S(1)}, u32[]{:S(2)}) copy-start(bf16[128,256]{1,0:T(8,128)(2,1)S(1)} %get-tuple-element.98) | copy-start | bytes 196612
  17.9 16.2 %copy-start.51 = (bf16[128,256]{1,0:T(8,128)(2,1)}, bf16[128,256]{1,0:T(8,128)(2,1)S(1)}, u32[]{:S(2)}) copy-start(bf16[128,256]{1,0:T(8,128)(2,1)S(1)} %get-tuple-element.97) | copy-start | bytes 196612
  17.9 16.2 %copy-start.53 = (bf16[128,256]{1,0:T(8,128)(2,1)}, bf16[128,256]{1,0:T(8,128)(2,1)S(1)}, u32[]{:S(2)}) copy-start(bf16[128,256]{1,0:T(8,128)(2,1)S(1)} %get-tuple-element.99) | copy-start | bytes 196612
  28.1 5.9 %collective-permute-start.6 = (bf16[2,1024,128]{2,1,0:T(8,128)(2,1)S(1)}, bf16[2,1024,128]{2,1,0:T(8,128)(2,1)S(1)}, u32[]{:S(2)}, u32[]{:S(2)}) collective-permute-start(bf16[2,1024,128]{2,1,0:T(8,128)(2,1)S(1)} %collective-permute-done.5), channel_id=1, source_target_pairs={{0,1},{1,0},{2,3},{3,2},{4,5},{5,4},{6,7},{7,6},{8,9},{9,8},{10,11... | collective-permute-start | bytes 1572872 | tf_op jit(solution)/shard_map/ppermute | solution.py:113
  30.4 21.4 %copy-start.41 = (bf16[1,1024,128]{2,1,0:T(8,128)(2,1)}, bf16[1,1024,128]{2,1,0:T(8,128)(2,1)S(1)}, u32[]{:S(2)}) copy-start(bf16[1,1024,128]{2,1,0:T(8,128)(2,1)S(1)} %slice.562) | copy-start | bytes 786436
  30.4 9.7 %collective-permute-start.3 = (bf16[1,1024,128]{2,1,0:T(8,128)(2,1)S(1)}, bf16[1,1024,128]{2,1,0:T(8,128)(2,1)S(1)}, u32[]{:S(2)}, u32[]{:S(2)}) collective-permute-start(bf16[1,1024,128]{2,1,0:T(8,128)(2,1)S(1)} %slice.562), channel_id=1, source_target_pairs={{0,4},{4,8},{8,12},{12,16},{16,20},{20,24},{24,28},{1,5},{5,9},{9,... | collective-permute-start | bytes 786440 | tf_op jit(solution)/shard_map/ppermute | solution.py:73
  41.1 16.9 %copy-start.27 = (bf16[2,1024,128]{2,1,0:T(8,128)(2,1)}, bf16[2,1024,128]{2,1,0:T(8,128)(2,1)S(1)}, u32[]{:S(2)}) copy-start(bf16[2,1024,128]{2,1,0:T(8,128)(2,1)S(1)} %get-tuple-element.87) | copy-start | bytes 1572868
  41.3 16.7 %copy-start.23 = (bf16[1,1024,128]{2,1,0:T(8,128)(2,1)}, bf16[1,1024,128]{2,1,0:T(8,128)(2,1)S(1)}, u32[]{:S(2)}) copy-start(bf16[1,1024,128]{2,1,0:T(8,128)(2,1)S(1)} %get-tuple-element.88) | copy-start | bytes 786436
  41.4 16.7 %copy-start.25 = (bf16[1,1024,128]{2,1,0:T(8,128)(2,1)}, bf16[1,1024,128]{2,1,0:T(8,128)(2,1)S(1)}, u32[]{:S(2)}) copy-start(bf16[1,1024,128]{2,1,0:T(8,128)(2,1)S(1)} %get-tuple-element.90) | copy-start | bytes 786436
  41.4 16.7 %copy-start.45 = (bf16[1,1024,128]{2,1,0:T(8,128)(2,1)}, bf16[1,1024,128]{2,1,0:T(8,128)(2,1)S(1)}, u32[]{:S(2)}) copy-start(bf16[1,1024,128]{2,1,0:T(8,128)(2,1)S(1)} %get-tuple-element.91) | copy-start | bytes 786436
  41.4 10.4 %collective-permute-start.7 = (bf16[1,1024,128]{2,1,0:T(8,128)(2,1)S(1)}, bf16[1,1024,128]{2,1,0:T(8,128)(2,1)S(1)}, u32[]{:S(2)}, u32[]{:S(2)}) collective-permute-start(bf16[1,1024,128]{2,1,0:T(8,128)(2,1)S(1)} %get-tuple-element.91), channel_id=1, source_target_pairs={{4,0},{8,4},{12,8},{16,12},{20,16},{24,20},{28,24},{5,1},{9,5},{13... | collective-permute-start | bytes 786440 | tf_op jit(solution)/shard_map/ppermute | solution.py:74
  42.7 15.4 %copy-start.64 = (f32[128]{0:T(128)}, f32[128]{0:T(128)S(1)}, u32[]{:S(2)}) copy-start(f32[128]{0:T(128)S(1)} %get-tuple-element.120) | copy-start | bytes 1540
  42.7 15.3 %copy-start.66 = (f32[128]{0:T(128)}, f32[128]{0:T(128)S(1)}, u32[]{:S(2)}) copy-start(f32[128]{0:T(128)S(1)} %get-tuple-element.121) | copy-start | bytes 1540
  42.7 15.3 %copy-start.68 = (f32[128]{0:T(128)}, f32[128]{0:T(128)S(1)}, u32[]{:S(2)}) copy-start(f32[128]{0:T(128)S(1)} %get-tuple-element.122) | copy-start | bytes 1540
  42.7 15.3 %copy-start.70 = (f32[128]{0:T(128)}, f32[128]{0:T(128)S(1)}, u32[]{:S(2)}) copy-start(f32[128]{0:T(128)S(1)} %get-tuple-element.123) | copy-start | bytes 1540
  42.7 15.3 %copy-start.72 = (f32[128]{0:T(128)}, f32[128]{0:T(128)S(1)}, u32[]{:S(2)}) copy-start(f32[128]{0:T(128)S(1)} %get-tuple-element.124) | copy-start | bytes 1540
  42.7 15.3 %copy-start.74 = (f32[128]{0:T(128)}, f32[128]{0:T(128)S(1)}, u32[]{:S(2)}) copy-start(f32[128]{0:T(128)S(1)} %get-tuple-element.125) | copy-start | bytes 1540
  42.8 32.5 %copy-start.57 = (f32[128]{0:T(128)}, f32[128]{0:T(128)S(1)}, u32[]{:S(2)}) copy-start(f32[128]{0:T(128)S(1)} %get-tuple-element.137) | copy-start | bytes 1540
  42.8 20.3 %collective-permute-start.8 = (bf16[1,1024,128]{2,1,0:T(8,128)(2,1)S(1)}, bf16[1,1024,128]{2,1,0:T(8,128)(2,1)S(1)}, u32[]{:S(2)}, u32[]{:S(2)}) collective-permute-start(bf16[1,1024,128]{2,1,0:T(8,128)(2,1)S(1)} %get-tuple-element.90), channel_id=1, source_target_pairs={{0,4},{4,8},{8,12},{12,16},{16,20},{20,24},{24,28},{1,5},{5,9},{9,... | collective-permute-start | bytes 786440 | tf_op jit(solution)/shard_map/ppermute | solution.py:73
  47.8 15.3 %collective-permute-start.9 = (bf16[1,1024,128]{2,1,0:T(8,128)(2,1)S(1)}, bf16[1,1024,128]{2,1,0:T(8,128)(2,1)S(1)}, u32[]{:S(2)}, u32[]{:S(2)}) collective-permute-start(bf16[1,1024,128]{2,1,0:T(8,128)(2,1)S(1)} %get-tuple-element.88), channel_id=1, source_target_pairs={{4,0},{8,4},{12,8},{16,12},{20,16},{24,20},{28,24},{5,1},{9,5},{13... | collective-permute-start | bytes 786440 | tf_op jit(solution)/shard_map/ppermute | solution.py:74
  65.7 32.0 %all-to-all-start = ((bf16[4,1024,128]{2,0,1:T(4,128)(2,1)}), bf16[4,1024,128]{2,0,1:T(4,128)(2,1)S(1)}, u32[]{:S(2)}, u32[]{:S(2)}) async-start(bf16[4,1024,128]{2,0,1:T(4,128)(2,1)} %copy.57), calls=%async_computation | async-start | bytes 2097152 | tf_op jit(solution)/shard_map/all_to_all | solution.py:192
  102.8 30.4 %copy-start.59 = (bf16[32,32,1]{0,1,2:T(8,128)(2,1)S(1)}, bf16[32,32,1]{0,1,2:T(8,128)(2,1)}, u32[]{:S(2)}) copy-start(bf16[32,32,1]{0,1,2:T(8,128)(2,1)} %constant.195) | copy-start | bytes 6148
  102.8 29.1 %all-to-all-start.2 = ((bf16[4,1024,128]{2,0,1:T(4,128)(2,1)}), bf16[4,1024,128]{2,0,1:T(4,128)(2,1)}, u32[]{:S(2)}, u32[]{:S(2)}) async-start(bf16[4,1024,128]{2,0,1:T(4,128)(2,1)} %copy.63), calls=%async_computation.2 | async-start | bytes 2097152 | tf_op jit(solution)/shard_map/all_to_all | solution.py:192
  138.9 29.7 %all-to-all-start.3 = ((bf16[32,128,128]{2,1,0:T(8,128)(2,1)}), bf16[32,128,128]{2,1,0:T(8,128)(2,1)}, u32[]{:S(2)}, u32[]{:S(2)}) async-start(bf16[32,128,128]{2,1,0:T(8,128)(2,1)} %copy.67), calls=%async_computation.3 | async-start | bytes 2097152 | tf_op jit(solution)/shard_map/all_to_all | solution.py:196
  145.9 26.5 %copy-start.63 = (bf16[32,32]{0,1:T(8,128)(2,1)S(1)}, bf16[32,32]{0,1:T(8,128)(2,1)}, u32[]{:S(2)}) copy-start(bf16[32,32]{0,1:T(8,128)(2,1)} %constant.169.clone) | copy-start | bytes 6148
  168.6 29.5 %all-to-all-start.1 = ((bf16[32,128,128]{2,1,0:T(8,128)(2,1)}), bf16[32,128,128]{2,1,0:T(8,128)(2,1)S(1)}, u32[]{:S(2)}, u32[]{:S(2)}) async-start(bf16[32,128,128]{2,1,0:T(8,128)(2,1)} %copy.60), calls=%async_computation.1 | async-start | bytes 2097152 | tf_op jit(solution)/shard_map/all_to_all | solution.py:196
  215.4 35.0 %copy-start.32 = (bf16[2,1024,128]{2,1,0:T(8,128)(2,1)}, bf16[2,1024,128]{2,1,0:T(8,128)(2,1)S(1)}, u32[]{:S(2)}) copy-start(bf16[2,1024,128]{2,1,0:T(8,128)(2,1)S(1)} %add_convert_fusion.1) | copy-start | bytes 1572868
  215.7 21.5 %collective-permute-start.12 = (bf16[1,1024,128]{2,1,0:T(8,128)(2,1)}, bf16[1,1024,128]{2,1,0:T(8,128)(2,1)S(1)}, u32[]{:S(2)}, u32[]{:S(2)}) collective-permute-start(bf16[1,1024,128]{2,1,0:T(8,128)(2,1)} %get-tuple-element.83), channel_id=1, source_target_pairs={{0,4},{4,8},{8,12},{12,16},{16,20},{20,24},{24,28},{1,5},{5,9},{9,... | collective-permute-start | bytes 786440 | tf_op jit(solution)/shard_map/ppermute | solution.py:73
  218.9 19.1 %collective-permute-start.13 = (bf16[1,1024,128]{2,1,0:T(8,128)(2,1)}, bf16[1,1024,128]{2,1,0:T(8,128)(2,1)S(1)}, u32[]{:S(2)}, u32[]{:S(2)}) collective-permute-start(bf16[1,1024,128]{2,1,0:T(8,128)(2,1)} %get-tuple-element.84), channel_id=1, source_target_pairs={{4,0},{8,4},{12,8},{16,12},{20,16},{24,20},{28,24},{5,1},{9,5},{13... | collective-permute-start | bytes 786440 | tf_op jit(solution)/shard_map/ppermute | solution.py:74
  220.2 20.6 %collective-permute-start.10 = (bf16[1,1024,128]{2,1,0:T(8,128)(2,1)}, bf16[1,1024,128]{2,1,0:T(8,128)(2,1)S(1)}, u32[]{:S(2)}, u32[]{:S(2)}) collective-permute-start(bf16[1,1024,128]{2,1,0:T(8,128)(2,1)} %get-tuple-element.79), channel_id=1, source_target_pairs={{0,4},{4,8},{8,12},{12,16},{16,20},{20,24},{24,28},{1,5},{5,9},{9,... | collective-permute-start | bytes 786440 | tf_op jit(solution)/shard_map/ppermute | solution.py:73
  224.7 17.5 %collective-permute-start.11 = (bf16[1,1024,128]{2,1,0:T(8,128)(2,1)}, bf16[1,1024,128]{2,1,0:T(8,128)(2,1)S(1)}, u32[]{:S(2)}, u32[]{:S(2)}) collective-permute-start(bf16[1,1024,128]{2,1,0:T(8,128)(2,1)} %get-tuple-element.80), channel_id=1, source_target_pairs={{4,0},{8,4},{12,8},{16,12},{20,16},{24,20},{28,24},{5,1},{9,5},{13... | collective-permute-start | bytes 786440 | tf_op jit(solution)/shard_map/ppermute | solution.py:74
  228.7 31.7 %collective-permute-start.16 = (bf16[2,1024,256]{2,1,0:T(8,128)(2,1)}, bf16[2,1024,256]{2,1,0:T(8,128)(2,1)}, u32[]{:S(2)}, u32[]{:S(2)}) collective-permute-start(bf16[2,1024,256]{2,1,0:T(8,128)(2,1)} %convolution_convert_fusion.2), channel_id=1, source_target_pairs={{0,1},{1,0},{2,3},{3,2},{4,5},{5,4},{6,7},{7,6},{8,9},{9,8},{10,11... | collective-permute-start | bytes 3145736 | tf_op jit(solution)/shard_map/ppermute | solution.py:122
  244.6 19.4 %collective-permute-start.14 = (bf16[2,1024,256]{2,1,0:T(8,128)(2,1)}, bf16[2,1024,256]{2,1,0:T(8,128)(2,1)}, u32[]{:S(2)}, u32[]{:S(2)}) collective-permute-start(bf16[2,1024,256]{2,1,0:T(8,128)(2,1)} %convolution_convert_fusion.3), channel_id=1, source_target_pairs={{0,1},{1,0},{2,3},{3,2},{4,5},{5,4},{6,7},{7,6},{8,9},{9,8},{10,11... | collective-permute-start | bytes 3145736 | tf_op jit(solution)/shard_map/ppermute | solution.py:122
  256.6 19.8 %all-to-all-start.4 = ((bf16[8,278,128]{2,1,0:T(8,128)(2,1)}), bf16[8,278,128]{2,1,0:T(8,128)(2,1)S(1)}, u32[]{:S(2)}, u32[]{:S(2)}) async-start(bf16[8,278,128]{2,1,0:T(8,128)(2,1)} %concatenate.149), calls=%async_computation.4 | async-start | bytes 1146880 | tf_op jit(solution)/shard_map/all_to_all | solution.py:264
  262.5 16.5 %collective-permute-start.17 = (bf16[2,1024,128]{2,1,0:T(8,128)(2,1)S(1)}, bf16[2,1024,128]{2,1,0:T(8,128)(2,1)}, u32[]{:S(2)}, u32[]{:S(2)}) collective-permute-start(bf16[2,1024,128]{2,1,0:T(8,128)(2,1)S(1)} %slice.768), channel_id=1, source_target_pairs={{0,2},{1,3},{2,0},{3,1},{4,6},{5,7},{6,4},{7,5},{8,10},{9,11},{10,... | collective-permute-start | bytes 1572872 | tf_op jit(solution)/shard_map/ppermute | solution.py:127
  267.2 20.7 %collective-permute-start.15 = (bf16[2,1024,128]{2,1,0:T(8,128)(2,1)}, bf16[2,1024,128]{2,1,0:T(8,128)(2,1)}, u32[]{:S(2)}, u32[]{:S(2)}) collective-permute-start(bf16[2,1024,128]{2,1,0:T(8,128)(2,1)} %slice.769), channel_id=1, source_target_pairs={{0,2},{1,3},{2,0},{3,1},{4,6},{5,7},{6,4},{7,5},{8,10},{9,11},{10,... | collective-permute-start | bytes 1572872 | tf_op jit(solution)/shard_map/ppermute | solution.py:127
  (90 other events, 338.3 us)
where the time goes:
time: 292 us; the launch traced here: 290 us
  waiting for transfers between devices  126 us (43%)
  matrix products  56.1 us (19%)
  starting transfers between devices  52.2 us (18%)
  local copies, waits for them, and re-layouts  36.8 us (13%)
  other arithmetic  16.3 us (6%)
    dot_general x22, matrix products, dot(): jnp.einsum(spec, a.astype(bf16), b.astype(bf16), preferred_element_type=f32)  56.1 us
    all_to_all x2, waiting for transfers between devices, to_columns(): lax.all_to_all(spectrum, 'grid', split_axis=1, concat_axis=0, tiled=True)  37.9 us
    all_to_all x2, waiting for transfers between devices, to_rows(): lax.all_to_all(spectrum, 'grid', split_axis=0, concat_axis=1, tiled=True)  27.5 us
    ppermute x2, waiting for transfers between devices, gather(): lax.ppermute(value, 'ch', [(i, (i - 2 * hop) % size) for i in range(size)])  22.3 us
    ppermute x4, waiting for transfers between devices, neighbours(): before = lax.ppermute(last, 'grid', [(i, i + 1) for i in range(size - 1)])  19.6 us
    ppermute x4, starting transfers between devices, neighbours(): before = lax.ppermute(last, 'grid', [(i, i + 1) for i in range(size - 1)])  16.4 us
    all_to_all x2, starting transfers between devices, to_columns(): lax.all_to_all(spectrum, 'grid', split_axis=1, concat_axis=0, tiled=True)  12.8 us
    all_to_all x1, waiting for transfers between devices, local(): lax.all_to_all(packed, 'grid', split_axis=0, concat_axis=0, tiled=True)  8.7 us
  transfers between devices with their start and end apart: 23, of which 13 were waited for; matrix products, arithmetic and copies ran while one was open for 24% of the time, Pallas kernels for 0%

commit v1 on v0

--- a/solution.py
+++ b/solution.py
@@ -189,17 +189,18 @@
         return dot("wk,rwc->rkc", wide, field).astype(bf16)
 
     def to_columns(spectrum):
-        return lax.all_to_all(spectrum, "grid", split_axis=1, concat_axis=0, tiled=True).astype(f32)
+        return lax.all_to_all(spectrum, "grid", split_axis=1, concat_axis=0, tiled=True)
 
     def to_rows(spectrum):
-        spectrum = (spectrum * wide_weight).astype(bf16)
-        back = lax.all_to_all(spectrum, "grid", split_axis=0, concat_axis=1, tiled=True)
-        return dot("wk,rkc->rwc", wide, back)
+        return lax.all_to_all(spectrum, "grid", split_axis=0, concat_axis=1, tiled=True)
+
+    def from_spectrum(back):
+        return lax.optimization_barrier(dot("wk,rkc->rwc", wide, back).astype(bf16))
 
     value_rows, before_a, after_a = lax.optimization_barrier(
         (spectrum_of(value_bf), before_a, after_a)
     )
-    value_spec = to_columns(value_rows)
+    value_spec = to_columns(value_rows).astype(f32)
     gate_bf, framed_a = stencil(
         [before_a, edge_a[:1], *split_rows(mid_a), edge_a[1:], after_a], kernel[0], False
     )
@@ -212,35 +213,40 @@
     mixed_rows = times(value_spec, row_coef, 1)
     value_tall = dot("hk,hwc->kwc", tall, mixed_rows)
     mixed = dot("hk,kwc->hwc", tall, times(value_tall, col_coef, 0) * tall_weight[:, None])
-    mix_col = to_rows(mixed)
+    mixed = (mixed * wide_weight).astype(bf16)
+    mixed, grad_spec = lax.optimization_barrier((mixed, grad_spec))
+    grad_spec = grad_spec.astype(f32)
+    mix_col = from_spectrum(to_rows(mixed)).astype(f32)
 
     grad_tall = dot("hk,hwc->kwc", tall, grad_spec)
     grad_row = dot("hk,kwc->hwc", tall, times_conj(grad_tall, col_coef, 0) * tall_weight[:, None])
-    grad_value = to_rows(times_conj(grad_row, row_coef, 1)).astype(bf16)
+    grad_back = to_rows((times_conj(grad_row, row_coef, 1) * wide_weight).astype(bf16))
+    gated = (gate_feat * mix_col).astype(bf16)
+    grad_gate = (grad_out * mix_col).astype(bf16)
+    gate_halo = neighbours(grad_gate[-1:], grad_gate[:1])
+    grad_back, gate_halo = lax.optimization_barrier((grad_back, gate_halo))
+    grad_value = from_spectrum(grad_back)
+    value_halo = neighbours(grad_value[-1:], grad_value[:1])
 
     col_term = correlate(grad_tall * wide_weight, value_tall, 0, 1, True)
     col_grad = dot("mk,kc->mc", tall, col_term * tall_weight) * scale
     row_term = correlate(grad_row, value_spec, 1, 0, first)
     row_grad = dot("mk,kc->mc", wide_own, row_term * wide_weight) * scale
 
-    gated = (gate_feat * mix_col).astype(bf16)
-    grad_gate = (grad_out * mix_col).astype(bf16)
-
-    def back_parts(grad, filt):
-        before, after = neighbours(grad[-1:], grad[:1])
+    def back_parts(grad, halo, filt):
+        before, after = halo
         rows = split_rows(grad)
         middle_back, _ = stencil(rows, filt, True)
         top, _ = stencil([before, rows[0], rows[1]], filt, True)
         bottom, _ = stencil([rows[-2], rows[-1], after], filt, True)
         return middle_back, jnp.concatenate([top, bottom], axis=0)
 
-    mid_back_a, edge_back_a = back_parts(grad_gate, kernel[0])
-    mid_back_b, edge_back_b = back_parts(grad_value, kernel[1])
+    mid_back_a, edge_back_a = back_parts(grad_gate, gate_halo, kernel[0])
+    mid_back_b, edge_back_b = back_parts(grad_value, value_halo, kernel[1])
     mid_back = jnp.concatenate([mid_back_a, mid_back_b], axis=2)
     edge_back = jnp.concatenate([edge_back_a, edge_back_b], axis=2)
     mid_grad = scatter_sum(mid_back, mates, others)
     edge_grad = scatter_sum(edge_back, mates, others)
-    input_grad = jnp.concatenate([edge_grad[:1], mid_grad, edge_grad[1:]], axis=0)
 
     gate_term = dot("rwd,rwc->dc", middle, mid_back_a) + dot("rwd,rwc->dc", edges, edge_back_a)
     value_term = dot("rwd,rwc->dc", middle, mid_back_b) + dot("rwd,rwc->dc", edges, edge_back_b)
@@ -261,7 +267,9 @@
         ],
         axis=1,
     ).astype(bf16)
+    packed, mid_grad = lax.optimization_barrier((packed, mid_grad))
     arrived = lax.all_to_all(packed, "grid", split_axis=0, concat_axis=0, tiled=True)
+    input_grad = jnp.concatenate([edge_grad[:1], mid_grad, edge_grad[1:]], axis=0)
     total = jnp.sum(arrived.astype(f32), axis=0)
     ends = np.cumsum([depth // tiles, depth // tiles, per, height // tiles])
     gate_grad, value_grad, row_share, col_share, short_sum = jnp.split(total, ends, axis=0)

time: 292 us -> 291 us (level)
  matrix products: 56.1 us -> 41.1 us
  other arithmetic: 16.3 us -> 30.9 us
  waiting for transfers between devices: 126 us -> 116 us
  starting transfers between devices: 52.2 us -> 58.3 us
  local copies, waits for them, and re-layouts: 36.8 us -> 40.4 us
    dot_general x22, matrix products: 56.1 us -> 41.1 us  [dot(): jnp.einsum(spec, a.astype(bf16), b.astype(bf16), preferred_element_type=f32)]
    reduce_sum x0 -> x2, other arithmetic: none -> 9.9 us  [filter_sums(): jnp.sum(grad * framed[i:i + rows, j:j + width].astype(f32), axis=(0, 1))]
    ppermute x4, waiting for transfers between devices: 19.6 us -> 13.4 us  [neighbours(): before = lax.ppermute(last, 'grid', [(i, i + 1) for i in range(size - 1)])]
    all_to_all x2, waiting for transfers between devices: 37.9 us -> 33.1 us  [to_columns(): lax.all_to_all(spectrum, 'grid', split_axis=1, concat_axis=0, tiled=True)]
    all_to_all x2, starting transfers between devices: 12.8 us -> 16.9 us  [to_columns(): lax.all_to_all(spectrum, 'grid', split_axis=1, concat_axis=0, tiled=True)]
    unnamed x239 -> x205, local copies, waits for them, and re-layouts: 5.25 us -> 6.54 us
  transfers between devices with their start and end apart: 23 -> 23, of which waited for: 13 -> 13; matrix products, arithmetic and copies ran while one was open for 24% -> 30% of each run, Pallas kernels for 0% -> 0%
where the time goes in v1:
time: 291 us; the launch traced here: 289 us
  waiting for transfers between devices  116 us (40%)
  starting transfers between devices  58.3 us (20%)
  matrix products  41.1 us (14%)
  local copies, waits for them, and re-layouts  40.4 us (14%)
  other arithmetic  30.9 us (11%)
    dot_general x22, matrix products, dot(): jnp.einsum(spec, a.astype(bf16), b.astype(bf16), preferred_element_type=f32)  41.1 us
    all_to_all x2, waiting for transfers between devices, to_columns(): lax.all_to_all(spectrum, 'grid', split_axis=1, concat_axis=0, tiled=True)  33.1 us
    all_to_all x2, waiting for transfers between devices, to_rows(): lax.all_to_all(spectrum, 'grid', split_axis=0, concat_axis=1, tiled=True)  28 us
    ppermute x2, waiting for transfers between devices, gather(): lax.ppermute(value, 'ch', [(i, (i - 2 * hop) % size) for i in range(size)])  21.6 us
    ppermute x4, starting transfers between devices, neighbours(): before = lax.ppermute(last, 'grid', [(i, i + 1) for i in range(size - 1)])  17 us
    all_to_all x2, starting transfers between devices, to_columns(): lax.all_to_all(spectrum, 'grid', split_axis=1, concat_axis=0, tiled=True)  16.9 us
    ppermute x4, waiting for transfers between devices, neighbours(): before = lax.ppermute(last, 'grid', [(i, i + 1) for i in range(size - 1)])  13.4 us
    convert_element_type x7, other arithmetic, stencil(): return (total.astype(bf16), framed)  10.7 us
  transfers between devices with their start and end apart: 23, of which 13 were waited for; matrix products, arithmetic and copies ran while one was open for 30% of the time, Pallas kernels for 0%

profile of v1, /device:TPU:0, one launch (start us, length us, event | category | flops | bytes accessed | tf_op | source)
XLA Modules:
  0.0 288.9 jit_solution(8126257498536275172)
XLA Ops:
  1.9 3.0 %collective-permute-start.1 = (bf16[2,1024,128]{2,1,0:T(8,128)(2,1)S(1)}, bf16[2,1024,128]{2,1,0:T(8,128)(2,1)S(1)}, u32[]{:S(2)}, u32[]{:S(2)}) collective-permute-start(bf16[2,1024,128]{2,1,0:T(8,128)(2,1)S(1)} %pad_maximum_fusion.14), channel_id=1, source_target_pairs={{0,2},{1,3},{2,0},{3,1},{4,6},{5,7},{6,4},{7,5},{8,10},{9,11},{10,... | collective-permute-start | bytes 1572872 | tf_op jit(solution)/shard_map/ppermute | solution.py:108
  5.8 11.9 %collective-permute-done.1 = bf16[2,1024,128]{2,1,0:T(8,128)(2,1)S(1)} collective-permute-done((bf16[2,1024,128]{2,1,0:T(8,128)(2,1)S(1)}, bf16[2,1024,128]{2,1,0:T(8,128)(2,1)S(1)}, u32[]{:S(2)}, u32[]{:S(2)}) %collective-permute-start.1) | collective-permute-done | bytes 524320 | tf_op jit(solution)/shard_map/ppermute | solution.py:108
  18.5 9.7 %collective-permute-done.5 = bf16[2,1024,128]{2,1,0:T(8,128)(2,1)} collective-permute-done((bf16[2,1024,128]{2,1,0:T(8,128)(2,1)S(1)}, bf16[2,1024,128]{2,1,0:T(8,128)(2,1)}, u32[]{:S(2)}, u32[]{:S(2)}) %collective-permute-start.5) | collective-permute-done | bytes 524320 | tf_op jit(solution)/shard_map/ppermute | solution.py:108
  28.3 1.9 convolution_convert_fusion.1
  30.3 3.6 %collective-permute-start.3 = (bf16[1,1024,128]{2,1,0:T(8,128)(2,1)S(1)}, bf16[1,1024,128]{2,1,0:T(8,128)(2,1)S(1)}, u32[]{:S(2)}, u32[]{:S(2)}) collective-permute-start(bf16[1,1024,128]{2,1,0:T(8,128)(2,1)S(1)} %slice.562), channel_id=1, source_target_pairs={{0,4},{4,8},{8,12},{12,16},{16,20},{20,24},{24,28},{1,5},{5,9},{9,... | collective-permute-start | bytes 786440 | tf_op jit(solution)/shard_map/ppermute | solution.py:73
  34.0 2.1 convolution_convert_fusion
  36.2 4.0 %collective-permute-done.3 = bf16[1,1024,128]{2,1,0:T(8,128)(2,1)S(1)} collective-permute-done((bf16[1,1024,128]{2,1,0:T(8,128)(2,1)S(1)}, bf16[1,1024,128]{2,1,0:T(8,128)(2,1)S(1)}, u32[]{:S(2)}, u32[]{:S(2)}) %collective-permute-start.3) | collective-permute-done | bytes 262176 | tf_op jit(solution)/shard_map/ppermute | solution.py:73
  44.7 5.0 %collective-permute-start.8 = (bf16[1,1024,128]{2,1,0:T(8,128)(2,1)S(1)}, bf16[1,1024,128]{2,1,0:T(8,128)(2,1)S(1)}, u32[]{:S(2)}, u32[]{:S(2)}) collective-permute-start(bf16[1,1024,128]{2,1,0:T(8,128)(2,1)S(1)} %get-tuple-element.100), channel_id=1, source_target_pairs={{0,4},{4,8},{8,12},{12,16},{16,20},{20,24},{24,28},{1,5},{5,9},{9,... | collective-permute-start | bytes 786440 | tf_op jit(solution)/shard_map/ppermute | solution.py:73
  51.0 2.6 collective-permute-done.7
  53.6 1.7 constant_dynamic-update-slice_fusion.2
  55.3 9.2 %fusion.43 = bf16[4,1024,128]{1,2,0:T(8,128)(2,1)} fusion(bf16[1024,1024,1]{1,0,2:T(8,128)(2,1)} %constant.190, f32[128]{0:T(128)S(1)} %get-tuple-element.131, f32[128]{0:T(128)S(1)} %get-tuple-element.132, f32[128]{0:T(128)} %get-tuple-element.133, f32[128]{0:T(128)} %get-tuple-element.134, f32[128]{0:T(128)} %get-tuple-element.135, ...), kind=kOutput, calls=%fused_computation.100 | convolution fusion | flops 1096286208 | bytes 6296064 | tf_op jit(solution)/shard_map/wk,rwc->rkc/dot_general | solution.py:68
  64.9 2.6 copy.57
  67.5 12.5 %all-to-all-start = ((bf16[4,1024,128]{2,0,1:T(4,128)(2,1)}), bf16[4,1024,128]{2,0,1:T(4,128)(2,1)S(1)}, u32[]{:S(2)}, u32[]{:S(2)}) async-start(bf16[4,1024,128]{2,0,1:T(4,128)(2,1)} %copy.57), calls=%async_computation | async-start | bytes 2097152 | tf_op jit(solution)/shard_map/all_to_all | solution.py:192
  81.5 3.3 %fusion.17 = bf16[4,1024,128]{2,1,0:T(8,128)(2,1)S(1)} fusion(f32[128]{0:T(128)S(1)} %get-tuple-element.140, f32[128]{0:T(128)S(1)} %get-tuple-element.141, f32[128]{0:T(128)S(1)} %get-tuple-element.142, f32[128]{0:T(128)S(1)} %get-tuple-element.143, f32[128]{0:T(128)S(1)} %get-tuple-element.144, f32[128]{0:T(128)S(1)} %get-tuple-element.145, ...), kind=kLoop, calls=%fused_computation.58 | loop fusion | flops 22020096 | bytes 4198912 | tf_op jit(solution)/shard_map/convert_element_type | solution.py:87
  84.8 2.3 fusion.44
  87.1 16.6 %all-to-all-done = bf16[4,1024,128]{2,0,1:T(4,128)(2,1)S(1)} async-done(((bf16[4,1024,128]{2,0,1:T(4,128)(2,1)}), bf16[4,1024,128]{2,0,1:T(4,128)(2,1)S(1)}, u32[]{:S(2)}, u32[]{:S(2)}) %all-to-all-start) | async-done | bytes 1048608 | tf_op jit(solution)/shard_map/all_to_all | solution.py:192
  104.7 1.8 copy.58
  106.5 2.4 copy.60
  108.9 4.4 %all-to-all-start.1 = ((bf16[4,1024,128]{2,0,1:T(4,128)(2,1)}), bf16[4,1024,128]{2,0,1:T(4,128)(2,1)}, u32[]{:S(2)}, u32[]{:S(2)}) async-start(bf16[4,1024,128]{2,0,1:T(4,128)(2,1)} %copy.60), calls=%async_computation.1 | async-start | bytes 2097152 | tf_op jit(solution)/shard_map/all_to_all | solution.py:192
  121.4 16.4 %all-to-all-done.1 = bf16[4,1024,128]{2,0,1:T(4,128)(2,1)} async-done(((bf16[4,1024,128]{2,0,1:T(4,128)(2,1)}), bf16[4,1024,128]{2,0,1:T(4,128)(2,1)}, u32[]{:S(2)}, u32[]{:S(2)}) %all-to-all-start.1) | async-done | bytes 1048608 | tf_op jit(solution)/shard_map/all_to_all | solution.py:192
  137.8 2.6 copy.61
  141.8 4.2 %all-to-all-start.2 = ((bf16[32,128,128]{2,1,0:T(8,128)(2,1)}), bf16[32,128,128]{2,1,0:T(8,128)(2,1)}, u32[]{:S(2)}, u32[]{:S(2)}) async-start(bf16[32,128,128]{2,1,0:T(8,128)(2,1)} %copy.62), calls=%async_computation.2 | async-start | bytes 2097152 | tf_op jit(solution)/shard_map/all_to_all | solution.py:195
  146.1 1.6 fusion.120
  152.4 1.9 fusion.48
  154.4 17.2 %all-to-all-done.2 = bf16[32,128,128]{2,1,0:T(8,128)(2,1)} async-done(((bf16[32,128,128]{2,1,0:T(8,128)(2,1)}), bf16[32,128,128]{2,1,0:T(8,128)(2,1)}, u32[]{:S(2)}, u32[]{:S(2)}) %all-to-all-start.2) | async-done | bytes 1048608 | tf_op jit(solution)/shard_map/all_to_all | solution.py:195
  171.5 3.6 %all-to-all-start.3 = ((bf16[32,128,128]{2,1,0:T(8,128)(2,1)}), bf16[32,128,128]{2,1,0:T(8,128)(2,1)S(1)}, u32[]{:S(2)}, u32[]{:S(2)}) async-start(bf16[32,128,128]{2,1,0:T(8,128)(2,1)} %copy.66), calls=%async_computation.3 | async-start | bytes 2097152 | tf_op jit(solution)/shard_map/all_to_all | solution.py:195
  175.9 1.7 copy.63
  178.9 3.3 %fusion.45 = bf16[4,1024,128]{2,1,0:T(8,128)(2,1)S(1)} fusion(bf16[4,1024,128]{1,2,0:T(8,128)(2,1)} %all_to_all.57, bf16[1024,1024,1]{1,0,2:T(8,128)(2,1)} %constant.190), kind=kOutput, calls=%fused_computation.102 | convolution fusion | flops 1074266112 | bytes 4194304 | tf_op jit(solution)/shard_map/wk,rkc->rwc/dot_general | solution.py:68
  182.3 5.0 %fusion.29 = (f32[128]{0:T(128)}, f32[128]{0:T(128)}, f32[128]{0:T(128)}, f32[128]{0:T(128)}, f32[128]{0:T(128)}, /*index=5*/f32[128]{0:T(128)}, f32[128]{0:T(12...) fusion(bf16[6,1024,128]{2,1,0:T(8,128)(2,1)S(1)} %copy-done.5, ...), kind=kLoop, calls=%fused_computation.70 | loop fusion | flops 26213248 | bytes 8393216 | tf_op jit(solution)/shard_map/reduce_sum | solution.py:98
  188.2 1.8 add_convert_fusion.1
  190.0 10.9 %all-to-all-done.3 = bf16[32,128,128]{2,1,0:T(8,128)(2,1)S(1)} async-done(((bf16[32,128,128]{2,1,0:T(8,128)(2,1)}), bf16[32,128,128]{2,1,0:T(8,128)(2,1)S(1)}, u32[]{:S(2)}, u32[]{:S(2)}) %all-to-all-start.3) | async-done | bytes 1048608 | tf_op jit(solution)/shard_map/all_to_all | solution.py:195
  202.1 3.5 %collective-permute-start.10 = (bf16[1,1024,128]{2,1,0:T(8,128)(2,1)}, bf16[1,1024,128]{2,1,0:T(8,128)(2,1)S(1)}, u32[]{:S(2)}, u32[]{:S(2)}) collective-permute-start(bf16[1,1024,128]{2,1,0:T(8,128)(2,1)} %get-tuple-element.93), channel_id=1, source_target_pairs={{0,4},{4,8},{8,12},{12,16},{16,20},{20,24},{24,28},{1,5},{5,9},{9,... | collective-permute-start | bytes 786440 | tf_op jit(solution)/shard_map/ppermute | solution.py:73
  207.2 9.0 %collective-permute-done.10 = bf16[1,1024,128]{2,1,0:T(8,128)(2,1)S(1)} collective-permute-done((bf16[1,1024,128]{2,1,0:T(8,128)(2,1)}, bf16[1,1024,128]{2,1,0:T(8,128)(2,1)S(1)}, u32[]{:S(2)}, u32[]{:S(2)}) %collective-permute-start.10) | collective-permute-done | bytes 262176 | tf_op jit(solution)/shard_map/ppermute | solution.py:73
  218.4 1.9 add_convert_fusion
  221.6 4.9 %collective-permute-start.12 = (bf16[1,1024,128]{2,1,0:T(8,128)(2,1)}, bf16[1,1024,128]{2,1,0:T(8,128)(2,1)S(1)}, u32[]{:S(2)}, u32[]{:S(2)}) collective-permute-start(bf16[1,1024,128]{2,1,0:T(8,128)(2,1)} %get-tuple-element.90), channel_id=1, source_target_pairs={{0,4},{4,8},{8,12},{12,16},{16,20},{20,24},{24,28},{1,5},{5,9},{9,... | collective-permute-start | bytes 786440 | tf_op jit(solution)/shard_map/ppermute | solution.py:73
  229.7 4.9 %fusion.38 = (f32[128]{0:T(128)}, f32[128]{0:T(128)}, f32[128]{0:T(128)}, f32[128]{0:T(128)}, f32[128]{0:T(128)}, /*index=5*/f32[128]{0:T(128)}, f32[128]{0:T(128)}, f32[128]{0:T(128)}, f32[128]{0:T(128)}) fusion(bf16[4,1024,128]{2,1,0:T(8,128)(2,1)S(1)} %fusion.46, bf16[6,1024,128]{2,1,0:T(8,128)(2,1)S(1)} %copy-done.24, ...), kind=kLoop, calls=%fused_computation.79 | loop fusion | flops 22543232 | bytes 4198912 | tf_op jit(solution)/shard_map/reduce_sum | solution.py:98
  234.7 2.1 stack.75
  238.5 1.9 convolution_bitcast_fusion.2
  240.4 2.0 fusion.50
  246.6 1.8 convolution_bitcast_fusion
  248.4 2.0 fusion.52
  251.1 1.6 collective-permute-start.17
  252.7 4.2 %concatenate.147 = bf16[8,278,128]{2,1,0:T(8,128)(2,1)} concatenate(bf16[8,64,128]{2,1,0:T(8,128)(2,1)S(1)} %bitcast.158, bf16[8,64,128]{2,1,0:T(8,128)(2,1)S(1)} %bitcast.159, bf16[8,128,128]{2,1,0:T(8,128)(2,1)S(1)} %bitcast.157, bf16[8,4,128]{2,1,0:T(4,128)(2,1)S(1)} %bitcast.168, bf16[8,18,128]{2,1,0:T(8,128)(2,1)S(1)} %broadcast_in_dim.12), dimensions={1} | concatenate | bytes 1138688 | tf_op jit(solution)/shard_map/concatenate | solution.py:260
  256.9 2.0 convert_add_fusion.1
  260.4 5.6 %collective-permute-done.17 = bf16[2,1024,128]{2,1,0:T(8,128)(2,1)} collective-permute-done((bf16[2,1024,128]{2,1,0:T(8,128)(2,1)S(1)}, bf16[2,1024,128]{2,1,0:T(8,128)(2,1)}, u32[]{:S(2)}, u32[]{:S(2)}) %collective-permute-start.17) | collective-permute-done | bytes 524320 | tf_op jit(solution)/shard_map/ppermute | solution.py:127
  267.2 5.0 %all-to-all-start.4 = ((bf16[8,278,128]{2,1,0:T(8,128)(2,1)}), bf16[8,278,128]{2,1,0:T(8,128)(2,1)S(1)}, u32[]{:S(2)}, u32[]{:S(2)}) async-start(bf16[8,278,128]{2,1,0:T(8,128)(2,1)} %concatenate.147), calls=%async_computation.4 | async-start | bytes 1146880 | tf_op jit(solution)/shard_map/all_to_all | solution.py:271
  272.1 4.4 %collective-permute-done.15 = bf16[2,1024,128]{2,1,0:T(8,128)(2,1)} collective-permute-done((bf16[2,1024,128]{2,1,0:T(8,128)(2,1)}, bf16[2,1024,128]{2,1,0:T(8,128)(2,1)}, u32[]{:S(2)}, u32[]{:S(2)}) %collective-permute-start.15) | collective-permute-done | bytes 524320 | tf_op jit(solution)/shard_map/ppermute | solution.py:127
  279.1 7.3 %all-to-all-done.4 = bf16[8,278,128]{2,1,0:T(8,128)(2,1)S(1)} async-done(((bf16[8,278,128]{2,1,0:T(8,128)(2,1)}), bf16[8,278,128]{2,1,0:T(8,128)(2,1)S(1)}, u32[]{:S(2)}, u32[]{:S(2)}) %all-to-all-start.4) | async-done | bytes 569376 | tf_op jit(solution)/shard_map/all_to_all | solution.py:271
  (298 shorter events, 51.9 us)
Async XLA Ops:
  0.6 115.2 %copy-start = (bf16[1024,128]{1,0:T(8,128)(2,1)S(1)}, bf16[1024,128]{1,0:T(8,128)(2,1)}, u32[]{:S(2)}) copy-start(bf16[1024,128]{1,0:T(8,128)(2,1)} %param.15) | copy-start | bytes 786436
  1.9 28.4 %copy-start.36 = (bf16[1,1024,128]{2,1,0:T(8,128)(2,1)}, bf16[1,1024,128]{2,1,0:T(8,128)(2,1)S(1)}, u32[]{:S(2)}) copy-start(bf16[1,1024,128]{2,1,0:T(8,128)(2,1)S(1)} %get-tuple-element.102) | copy-start | bytes 786436
  1.9 28.4 %copy-start.38 = (bf16[1,1024,128]{2,1,0:T(8,128)(2,1)}, bf16[1,1024,128]{2,1,0:T(8,128)(2,1)S(1)}, u32[]{:S(2)}) copy-start(bf16[1,1024,128]{2,1,0:T(8,128)(2,1)S(1)} %get-tuple-element.103) | copy-start | bytes 786436
  1.9 15.8 %collective-permute-start.1 = (bf16[2,1024,128]{2,1,0:T(8,128)(2,1)S(1)}, bf16[2,1024,128]{2,1,0:T(8,128)(2,1)S(1)}, u32[]{:S(2)}, u32[]{:S(2)}) collective-permute-start(bf16[2,1024,128]{2,1,0:T(8,128)(2,1)S(1)} %pad_maximum_fusion.14), channel_id=1, source_target_pairs={{0,2},{1,3},{2,0},{3,1},{4,6},{5,7},{6,4},{7,5},{8,10},{9,11},{10,... | collective-permute-start | bytes 1572872 | tf_op jit(solution)/shard_map/ppermute | solution.py:108
  5.0 23.3 %collective-permute-start = (bf16[2,1024,128]{2,1,0:T(8,128)(2,1)S(1)}, bf16[2,1024,128]{2,1,0:T(8,128)(2,1)}, u32[]{:S(2)}, u32[]{:S(2)}) collective-permute-start(bf16[2,1024,128]{2,1,0:T(8,128)(2,1)S(1)} %pad_maximum_fusion.14), channel_id=1, source_target_pairs={{0,1},{1,0},{2,3},{3,2},{4,5},{5,4},{6,7},{7,6},{8,9},{9,8},{10,11... | collective-permute-start | bytes 1572872 | tf_op jit(solution)/shard_map/ppermute | solution.py:113
  5.0 29.0 %copy-start.41 = (bf16[2,1024,128]{2,1,0:T(8,128)(2,1)}, bf16[2,1024,128]{2,1,0:T(8,128)(2,1)S(1)}, u32[]{:S(2)}) copy-start(bf16[2,1024,128]{2,1,0:T(8,128)(2,1)S(1)} %slice.469) | copy-start | bytes 1572868
  5.0 23.2 %collective-permute-start.5 = (bf16[2,1024,128]{2,1,0:T(8,128)(2,1)S(1)}, bf16[2,1024,128]{2,1,0:T(8,128)(2,1)}, u32[]{:S(2)}, u32[]{:S(2)}) collective-permute-start(bf16[2,1024,128]{2,1,0:T(8,128)(2,1)S(1)} %slice.469), channel_id=1, source_target_pairs={{0,2},{1,3},{2,0},{3,1},{4,6},{5,7},{6,4},{7,5},{8,10},{9,11},{10,... | collective-permute-start | bytes 1572872 | tf_op jit(solution)/shard_map/ppermute | solution.py:108
  5.2 28.8 %collective-permute-start.4 = (bf16[2,1024,128]{2,1,0:T(8,128)(2,1)S(1)}, bf16[2,1024,128]{2,1,0:T(8,128)(2,1)}, u32[]{:S(2)}, u32[]{:S(2)}) collective-permute-start(bf16[2,1024,128]{2,1,0:T(8,128)(2,1)S(1)} %slice.469), channel_id=1, source_target_pairs={{0,1},{1,0},{2,3},{3,2},{4,5},{5,4},{6,7},{7,6},{8,9},{9,8},{10,11... | collective-permute-start | bytes 1572872 | tf_op jit(solution)/shard_map/ppermute | solution.py:113
  17.7 12.5 %copy-start.92 = (bf16[2,1024,128]{2,1,0:T(8,128)(2,1)}, bf16[2,1024,128]{2,1,0:T(8,128)(2,1)S(1)}, u32[]{:S(2)}) copy-start(bf16[2,1024,128]{2,1,0:T(8,128)(2,1)S(1)} %collective-permute-done.1) | copy-start | bytes 1572868
  17.7 10.5 %collective-permute-start.2 = (bf16[2,1024,128]{2,1,0:T(8,128)(2,1)S(1)}, bf16[2,1024,128]{2,1,0:T(8,128)(2,1)S(1)}, u32[]{:S(2)}, u32[]{:S(2)}) collective-permute-start(bf16[2,1024,128]{2,1,0:T(8,128)(2,1)S(1)} %collective-permute-done.1), channel_id=1, source_target_pairs={{0,1},{1,0},{2,3},{3,2},{4,5},{5,4},{6,7},{7,6},{8,9},{9,8},{10,11... | collective-permute-start | bytes 1572872 | tf_op jit(solution)/shard_map/ppermute | solution.py:113
  17.8 16.2 %copy-start.55 = (bf16[128,256]{1,0:T(8,128)(2,1)}, bf16[128,256]{1,0:T(8,128)(2,1)S(1)}, u32[]{:S(2)}) copy-start(bf16[128,256]{1,0:T(8,128)(2,1)S(1)} %get-tuple-element.108) | copy-start | bytes 196612
  17.8 16.2 %copy-start.57 = (bf16[128,256]{1,0:T(8,128)(2,1)}, bf16[128,256]{1,0:T(8,128)(2,1)S(1)}, u32[]{:S(2)}) copy-start(bf16[128,256]{1,0:T(8,128)(2,1)S(1)} %get-tuple-element.107) | copy-start | bytes 196612
  17.8 16.2 %copy-start.59 = (bf16[128,256]{1,0:T(8,128)(2,1)}, bf16[128,256]{1,0:T(8,128)(2,1)S(1)}, u32[]{:S(2)}) copy-start(bf16[128,256]{1,0:T(8,128)(2,1)S(1)} %get-tuple-element.109) | copy-start | bytes 196612
  18.5 36.8 %copy-start.68 = (f32[128]{0:T(128)}, f32[128]{0:T(128)S(1)}, u32[]{:S(2)}) copy-start(f32[128]{0:T(128)S(1)} %get-tuple-element.130) | copy-start | bytes 1540
  18.5 36.8 %copy-start.70 = (f32[128]{0:T(128)}, f32[128]{0:T(128)S(1)}, u32[]{:S(2)}) copy-start(f32[128]{0:T(128)S(1)} %get-tuple-element.131) | copy-start | bytes 1540
  18.5 36.8 %copy-start.72 = (f32[128]{0:T(128)}, f32[128]{0:T(128)S(1)}, u32[]{:S(2)}) copy-start(f32[128]{0:T(128)S(1)} %get-tuple-element.132) | copy-start | bytes 1540
  28.2 5.7 %collective-permute-start.6 = (bf16[2,1024,128]{2,1,0:T(8,128)(2,1)}, bf16[2,1024,128]{2,1,0:T(8,128)(2,1)S(1)}, u32[]{:S(2)}, u32[]{:S(2)}) collective-permute-start(bf16[2,1024,128]{2,1,0:T(8,128)(2,1)} %collective-permute-done.5), channel_id=1, source_target_pairs={{0,1},{1,0},{2,3},{3,2},{4,5},{5,4},{6,7},{7,6},{8,9},{9,8},{10,11... | collective-permute-start | bytes 1572872 | tf_op jit(solution)/shard_map/ppermute | solution.py:113
  30.3 9.8 %collective-permute-start.3 = (bf16[1,1024,128]{2,1,0:T(8,128)(2,1)S(1)}, bf16[1,1024,128]{2,1,0:T(8,128)(2,1)S(1)}, u32[]{:S(2)}, u32[]{:S(2)}) collective-permute-start(bf16[1,1024,128]{2,1,0:T(8,128)(2,1)S(1)} %slice.562), channel_id=1, source_target_pairs={{0,4},{4,8},{8,12},{12,16},{16,20},{20,24},{24,28},{1,5},{5,9},{9,... | collective-permute-start | bytes 786440 | tf_op jit(solution)/shard_map/ppermute | solution.py:73
  33.9 47.4 %copy-start.62 = (f32[128]{0:T(128)}, f32[128]{0:T(128)S(1)}, u32[]{:S(2)}) copy-start(f32[128]{0:T(128)S(1)} %get-tuple-element.147) | copy-start | bytes 1540
  40.5 24.0 %copy-start.25 = (bf16[2,1024,128]{2,1,0:T(8,128)(2,1)}, bf16[2,1024,128]{2,1,0:T(8,128)(2,1)S(1)}, u32[]{:S(2)}) copy-start(bf16[2,1024,128]{2,1,0:T(8,128)(2,1)S(1)} %get-tuple-element.97) | copy-start | bytes 1572868
  40.5 40.9 %copy-start.8 = (bf16[2,1024,128]{2,1,0:T(8,128)(2,1)}, bf16[2,1024,128]{2,1,0:T(8,128)(2,1)S(1)}, u32[]{:S(2)}) copy-start(bf16[2,1024,128]{2,1,0:T(8,128)(2,1)S(1)} %get-tuple-element.95) | copy-start | bytes 1572868
  41.6 22.9 %copy-start.17 = (bf16[1,1024,128]{2,1,0:T(8,128)(2,1)}, bf16[1,1024,128]{2,1,0:T(8,128)(2,1)S(1)}, u32[]{:S(2)}) copy-start(bf16[1,1024,128]{2,1,0:T(8,128)(2,1)S(1)} %get-tuple-element.98) | copy-start | bytes 786436
  41.6 22.9 %copy-start.20 = (bf16[1,1024,128]{2,1,0:T(8,128)(2,1)}, bf16[1,1024,128]{2,1,0:T(8,128)(2,1)S(1)}, u32[]{:S(2)}) copy-start(bf16[1,1024,128]{2,1,0:T(8,128)(2,1)S(1)} %get-tuple-element.100) | copy-start | bytes 786436
  42.8 10.9 %collective-permute-start.7 = (bf16[1,1024,128]{2,1,0:T(8,128)(2,1)}, bf16[1,1024,128]{2,1,0:T(8,128)(2,1)}, u32[]{:S(2)}, u32[]{:S(2)}) collective-permute-start(bf16[1,1024,128]{2,1,0:T(8,128)(2,1)} %get-tuple-element.101), channel_id=1, source_target_pairs={{4,0},{8,4},{12,8},{16,12},{20,16},{24,20},{28,24},{5,1},{9,5},{13... | collective-permute-start | bytes 786440 | tf_op jit(solution)/shard_map/ppermute | solution.py:74
  44.7 20.2 %collective-permute-start.8 = (bf16[1,1024,128]{2,1,0:T(8,128)(2,1)S(1)}, bf16[1,1024,128]{2,1,0:T(8,128)(2,1)S(1)}, u32[]{:S(2)}, u32[]{:S(2)}) collective-permute-start(bf16[1,1024,128]{2,1,0:T(8,128)(2,1)S(1)} %get-tuple-element.100), channel_id=1, source_target_pairs={{0,4},{4,8},{8,12},{12,16},{16,20},{20,24},{24,28},{1,5},{5,9},{9,... | collective-permute-start | bytes 786440 | tf_op jit(solution)/shard_map/ppermute | solution.py:73
  49.7 15.2 %collective-permute-start.9 = (bf16[1,1024,128]{2,1,0:T(8,128)(2,1)S(1)}, bf16[1,1024,128]{2,1,0:T(8,128)(2,1)S(1)}, u32[]{:S(2)}, u32[]{:S(2)}) collective-permute-start(bf16[1,1024,128]{2,1,0:T(8,128)(2,1)S(1)} %get-tuple-element.98), channel_id=1, source_target_pairs={{4,0},{8,4},{12,8},{16,12},{20,16},{24,20},{28,24},{5,1},{9,5},{13... | collective-permute-start | bytes 786440 | tf_op jit(solution)/shard_map/ppermute | solution.py:74
  64.9 16.5 %copy-start.12 = (bf16[1,1024,128]{2,1,0:T(8,128)(2,1)}, bf16[1,1024,128]{2,1,0:T(8,128)(2,1)S(1)}, u32[]{:S(2)}) copy-start(bf16[1,1024,128]{2,1,0:T(8,128)(2,1)S(1)} %collective-permute-done.8) | copy-start | bytes 786436
  64.9 16.5 %copy-start.14 = (bf16[1,1024,128]{2,1,0:T(8,128)(2,1)}, bf16[1,1024,128]{2,1,0:T(8,128)(2,1)S(1)}, u32[]{:S(2)}) copy-start(bf16[1,1024,128]{2,1,0:T(8,128)(2,1)S(1)} %collective-permute-done.9) | copy-start | bytes 786436
  67.5 36.2 %all-to-all-start = ((bf16[4,1024,128]{2,0,1:T(4,128)(2,1)}), bf16[4,1024,128]{2,0,1:T(4,128)(2,1)S(1)}, u32[]{:S(2)}, u32[]{:S(2)}) async-start(bf16[4,1024,128]{2,0,1:T(4,128)(2,1)} %copy.57), calls=%async_computation | async-start | bytes 2097152 | tf_op jit(solution)/shard_map/all_to_all | solution.py:192
  108.9 28.9 %all-to-all-start.1 = ((bf16[4,1024,128]{2,0,1:T(4,128)(2,1)}), bf16[4,1024,128]{2,0,1:T(4,128)(2,1)}, u32[]{:S(2)}, u32[]{:S(2)}) async-start(bf16[4,1024,128]{2,0,1:T(4,128)(2,1)} %copy.60), calls=%async_computation.1 | async-start | bytes 2097152 | tf_op jit(solution)/shard_map/all_to_all | solution.py:192
  141.8 29.7 %all-to-all-start.2 = ((bf16[32,128,128]{2,1,0:T(8,128)(2,1)}), bf16[32,128,128]{2,1,0:T(8,128)(2,1)}, u32[]{:S(2)}, u32[]{:S(2)}) async-start(bf16[32,128,128]{2,1,0:T(8,128)(2,1)} %copy.62), calls=%async_computation.2 | async-start | bytes 2097152 | tf_op jit(solution)/shard_map/all_to_all | solution.py:195
  151.9 23.1 %copy-start.67 = (bf16[32,32]{0,1:T(8,128)(2,1)S(1)}, bf16[32,32]{0,1:T(8,128)(2,1)}, u32[]{:S(2)}) copy-start(bf16[32,32]{0,1:T(8,128)(2,1)} %constant.169.clone) | copy-start | bytes 6148
  171.5 29.3 %all-to-all-start.3 = ((bf16[32,128,128]{2,1,0:T(8,128)(2,1)}), bf16[32,128,128]{2,1,0:T(8,128)(2,1)S(1)}, u32[]{:S(2)}, u32[]{:S(2)}) async-start(bf16[32,128,128]{2,1,0:T(8,128)(2,1)} %copy.66), calls=%async_computation.3 | async-start | bytes 2097152 | tf_op jit(solution)/shard_map/all_to_all | solution.py:195
  202.0 14.2 %copy-start.28 = (bf16[1024,1024,1]{1,0,2:T(8,128)(2,1)S(1)}, bf16[1024,1024,1]{1,0,2:T(8,128)(2,1)}, u32[]{:S(2)}) copy-start(bf16[1024,1024,1]{1,0,2:T(8,128)(2,1)} %constant.190) | copy-start | bytes 6291460
  202.1 14.2 %collective-permute-start.10 = (bf16[1,1024,128]{2,1,0:T(8,128)(2,1)}, bf16[1,1024,128]{2,1,0:T(8,128)(2,1)S(1)}, u32[]{:S(2)}, u32[]{:S(2)}) collective-permute-start(bf16[1,1024,128]{2,1,0:T(8,128)(2,1)} %get-tuple-element.93), channel_id=1, source_target_pairs={{0,4},{4,8},{8,12},{12,16},{16,20},{20,24},{24,28},{1,5},{5,9},{9,... | collective-permute-start | bytes 786440 | tf_op jit(solution)/shard_map/ppermute | solution.py:73
  205.5 10.7 %collective-permute-start.11 = (bf16[1,1024,128]{2,1,0:T(8,128)(2,1)}, bf16[1,1024,128]{2,1,0:T(8,128)(2,1)S(1)}, u32[]{:S(2)}, u32[]{:S(2)}) collective-permute-start(bf16[1,1024,128]{2,1,0:T(8,128)(2,1)} %get-tuple-element.92), channel_id=1, source_target_pairs={{4,0},{8,4},{12,8},{16,12},{20,16},{24,20},{28,24},{5,1},{9,5},{13... | collective-permute-start | bytes 786440 | tf_op jit(solution)/shard_map/ppermute | solution.py:74
  207.1 11.2 %copy-start.69 = (f32[128]{0:T(128)S(1)}, f32[128]{0:T(128)}, u32[]{:S(2)}) copy-start(f32[128]{0:T(128)} %copy-done.68) | copy-start | bytes 1540
  207.1 11.2 %copy-start.71 = (f32[128]{0:T(128)S(1)}, f32[128]{0:T(128)}, u32[]{:S(2)}) copy-start(f32[128]{0:T(128)} %copy-done.70) | copy-start | bytes 1540
  207.2 11.2 %copy-start.73 = (f32[128]{0:T(128)S(1)}, f32[128]{0:T(128)}, u32[]{:S(2)}) copy-start(f32[128]{0:T(128)} %copy-done.72) | copy-start | bytes 1540
  207.2 11.2 %copy-start.74 = (f32[128]{0:T(128)S(1)}, f32[128]{0:T(128)}, u32[]{:S(2)}) copy-start(f32[128]{0:T(128)} %get-tuple-element.133) | copy-start | bytes 1540
  220.3 22.8 %collective-permute-start.13 = (bf16[1,1024,128]{2,1,0:T(8,128)(2,1)}, bf16[1,1024,128]{2,1,0:T(8,128)(2,1)S(1)}, u32[]{:S(2)}, u32[]{:S(2)}) collective-permute-start(bf16[1,1024,128]{2,1,0:T(8,128)(2,1)} %get-tuple-element.91), channel_id=1, source_target_pairs={{4,0},{8,4},{12,8},{16,12},{20,16},{24,20},{28,24},{5,1},{9,5},{13... | collective-permute-start | bytes 786440 | tf_op jit(solution)/shard_map/ppermute | solution.py:74
  221.6 21.8 %collective-permute-start.12 = (bf16[1,1024,128]{2,1,0:T(8,128)(2,1)}, bf16[1,1024,128]{2,1,0:T(8,128)(2,1)S(1)}, u32[]{:S(2)}, u32[]{:S(2)}) collective-permute-start(bf16[1,1024,128]{2,1,0:T(8,128)(2,1)} %get-tuple-element.90), channel_id=1, source_target_pairs={{0,4},{4,8},{8,12},{12,16},{16,20},{20,24},{24,28},{1,5},{5,9},{9,... | collective-permute-start | bytes 786440 | tf_op jit(solution)/shard_map/ppermute | solution.py:73
  238.4 12.1 %collective-permute-start.16 = (bf16[2,1024,256]{2,1,0:T(8,128)(2,1)S(1)}, bf16[2,1024,256]{2,1,0:T(8,128)(2,1)S(1)}, u32[]{:S(2)}, u32[]{:S(2)}) collective-permute-start(bf16[2,1024,256]{2,1,0:T(8,128)(2,1)S(1)} %convolution_convert_fusion.2), channel_id=1, source_target_pairs={{0,1},{1,0},{2,3},{3,2},{4,5},{5,4},{6,7},{7,6},{8,9},{9,8},{10,11... | collective-permute-start | bytes 3145736 | tf_op jit(solution)/shard_map/ppermute | solution.py:122
  246.2 10.7 %collective-permute-start.14 = (bf16[2,1024,256]{2,1,0:T(8,128)(2,1)}, bf16[2,1024,256]{2,1,0:T(8,128)(2,1)}, u32[]{:S(2)}, u32[]{:S(2)}) collective-permute-start(bf16[2,1024,256]{2,1,0:T(8,128)(2,1)} %convolution_convert_fusion.3), channel_id=1, source_target_pairs={{0,1},{1,0},{2,3},{3,2},{4,5},{5,4},{6,7},{7,6},{8,9},{9,8},{10,11... | collective-permute-start | bytes 3145736 | tf_op jit(solution)/shard_map/ppermute | solution.py:122
  251.1 14.9 %collective-permute-start.17 = (bf16[2,1024,128]{2,1,0:T(8,128)(2,1)S(1)}, bf16[2,1024,128]{2,1,0:T(8,128)(2,1)}, u32[]{:S(2)}, u32[]{:S(2)}) collective-permute-start(bf16[2,1024,128]{2,1,0:T(8,128)(2,1)S(1)} %slice.768), channel_id=1, source_target_pairs={{0,2},{1,3},{2,0},{3,1},{4,6},{5,7},{6,4},{7,5},{8,10},{9,11},{10,... | collective-permute-start | bytes 1572872 | tf_op jit(solution)/shard_map/ppermute | solution.py:127
  259.8 16.6 %collective-permute-start.15 = (bf16[2,1024,128]{2,1,0:T(8,128)(2,1)}, bf16[2,1024,128]{2,1,0:T(8,128)(2,1)}, u32[]{:S(2)}, u32[]{:S(2)}) collective-permute-start(bf16[2,1024,128]{2,1,0:T(8,128)(2,1)} %slice.769), channel_id=1, source_target_pairs={{0,2},{1,3},{2,0},{3,1},{4,6},{5,7},{6,4},{7,5},{8,10},{9,11},{10,... | collective-permute-start | bytes 1572872 | tf_op jit(solution)/shard_map/ppermute | solution.py:127
  267.2 19.2 %all-to-all-start.4 = ((bf16[8,278,128]{2,1,0:T(8,128)(2,1)}), bf16[8,278,128]{2,1,0:T(8,128)(2,1)S(1)}, u32[]{:S(2)}, u32[]{:S(2)}) async-start(bf16[8,278,128]{2,1,0:T(8,128)(2,1)} %concatenate.147), calls=%async_computation.4 | async-start | bytes 1146880 | tf_op jit(solution)/shard_map/all_to_all | solution.py:271
  276.5 12.5 %copy-start.1 = (bf16[1024,128]{1,0:T(8,128)(2,1)S(1)}, bf16[1024,128]{1,0:T(8,128)(2,1)}, u32[]{:S(2)}) copy-start(bf16[1024,128]{1,0:T(8,128)(2,1)} %param.15) | copy-start | bytes 786436
  (73 other events, 267.8 us)

commit v2 on v1

--- a/solution.py
+++ b/solution.py
@@ -114,16 +114,22 @@
     return jnp.concatenate(blocks, axis=2)
 
 
-def scatter_sum(value, mates, others):
+def scatter_start(value, mates, others):
     size = lax.axis_size("ch")
     chips = size // 2
     channels = others.shape[1] // chips
     sent = dot("rwc,cd->rwd", value, mates).astype(bf16)
     got = lax.ppermute(sent, "ch", [(i, i ^ 1) for i in range(size)])
     pair = dot("rwc,cd->rwd", value, others) + got.astype(f32)
-    total = pair[..., :channels]
-    for hop in range(1, chips):
-        part = pair[..., hop * channels : (hop + 1) * channels].astype(bf16)
+    parts_out = [
+        pair[..., hop * channels : (hop + 1) * channels].astype(bf16) for hop in range(1, chips)
+    ]
+    return pair[..., :channels], parts_out
+
+
+def scatter_end(total, parts_out):
+    size = lax.axis_size("ch")
+    for hop, part in enumerate(parts_out, 1):
         total = total + lax.ppermute(
             part, "ch", [(i, (i + 2 * hop) % size) for i in range(size)]
         ).astype(f32)
@@ -224,7 +230,6 @@
     gated = (gate_feat * mix_col).astype(bf16)
     grad_gate = (grad_out * mix_col).astype(bf16)
     gate_halo = neighbours(grad_gate[-1:], grad_gate[:1])
-    grad_back, gate_halo = lax.optimization_barrier((grad_back, gate_halo))
     grad_value = from_spectrum(grad_back)
     value_halo = neighbours(grad_value[-1:], grad_value[:1])
 
@@ -233,20 +238,31 @@
     row_term = correlate(grad_row, value_spec, 1, 0, first)
     row_grad = dot("mk,kc->mc", wide_own, row_term * wide_weight) * scale
 
-    def back_parts(grad, halo, filt):
+    def middle_rows(grad, filt):
+        return stencil(split_rows(grad), filt, True)[0]
+
+    def edge_rows(grad, halo, filt):
         before, after = halo
         rows = split_rows(grad)
-        middle_back, _ = stencil(rows, filt, True)
         top, _ = stencil([before, rows[0], rows[1]], filt, True)
         bottom, _ = stencil([rows[-2], rows[-1], after], filt, True)
-        return middle_back, jnp.concatenate([top, bottom], axis=0)
-
-    mid_back_a, edge_back_a = back_parts(grad_gate, gate_halo, kernel[0])
-    mid_back_b, edge_back_b = back_parts(grad_value, value_halo, kernel[1])
+        return jnp.concatenate([top, bottom], axis=0)
+
+    mid_back_a = middle_rows(grad_gate, kernel[0])
+    mid_back_b = middle_rows(grad_value, kernel[1])
     mid_back = jnp.concatenate([mid_back_a, mid_back_b], axis=2)
+    mid_sum, mid_parts = scatter_start(mid_back, mates, others)
+    value_halo, mid_parts = lax.optimization_barrier((value_halo, mid_parts))
+    mid_grad = scatter_end(mid_sum, mid_parts)
+
+    edge_back_a = edge_rows(grad_gate, gate_halo, kernel[0])
+    edge_back_b = edge_rows(grad_value, value_halo, kernel[1])
     edge_back = jnp.concatenate([edge_back_a, edge_back_b], axis=2)
-    mid_grad = scatter_sum(mid_back, mates, others)
-    edge_grad = scatter_sum(edge_back, mates, others)
+    edge_sum, edge_parts = scatter_start(edge_back, mates, others)
+    edge_back_a, edge_back_b, edge_parts = lax.optimization_barrier(
+        (edge_back_a, edge_back_b, edge_parts)
+    )
+    edge_grad = scatter_end(edge_sum, edge_parts)
 
     gate_term = dot("rwd,rwc->dc", middle, mid_back_a) + dot("rwd,rwc->dc", edges, edge_back_a)
     value_term = dot("rwd,rwc->dc", middle, mid_back_b) + dot("rwd,rwc->dc", edges, edge_back_b)

time: 291 us -> 281 us (0.966)
  waiting for transfers between devices: 116 us -> 108 us
  other arithmetic: 30.9 us -> 27.7 us
    all_to_all x2, waiting for transfers between devices: 33.1 us -> 26.8 us  [to_columns(): lax.all_to_all(spectrum, 'grid', split_axis=1, concat_axis=0, tiled=True)]
    ppermute x4, waiting for transfers between devices: 9.99 us -> 6.25 us  [the longest x2 6.25 us: scatter_end(): lax.ppermute(part, 'ch', [(i, (i + 2 * hop) % size) for i in range(size)])]
    all_to_all x1, waiting for transfers between devices: 7.27 us -> 11 us  [local(): lax.all_to_all(packed, 'grid', split_axis=0, concat_axis=0, tiled=True)]
    unnamed x205 -> x203, local copies, waits for them, and re-layouts: 6.54 us -> 6.73 us
  transfers between devices with their start and end apart: 23 -> 23, of which waited for: 13 -> 13; matrix products, arithmetic and copies ran while one was open for 30% -> 25% of each run, Pallas kernels for 0% -> 0%
where the time goes in v2:
time: 281 us; the launch traced here: 279 us
  waiting for transfers between devices  108 us (38%)
  starting transfers between devices  60 us (21%)
  matrix products  41.8 us (15%)
  local copies, waits for them, and re-layouts  39.7 us (14%)
  other arithmetic  27.7 us (10%)
    dot_general x22, matrix products, dot(): jnp.einsum(spec, a.astype(bf16), b.astype(bf16), preferred_element_type=f32)  41.8 us
    all_to_all x2, waiting for transfers between devices, to_columns(): lax.all_to_all(spectrum, 'grid', split_axis=1, concat_axis=0, tiled=True)  26.8 us
    all_to_all x2, waiting for transfers between devices, to_rows(): lax.all_to_all(spectrum, 'grid', split_axis=0, concat_axis=1, tiled=True)  25.2 us
    ppermute x2, waiting for transfers between devices, gather(): lax.ppermute(value, 'ch', [(i, (i - 2 * hop) % size) for i in range(size)])  21.7 us
    ppermute x4, starting transfers between devices, neighbours(): before = lax.ppermute(last, 'grid', [(i, i + 1) for i in range(size - 1)])  18 us
    all_to_all x2, starting transfers between devices, to_columns(): lax.all_to_all(spectrum, 'grid', split_axis=1, concat_axis=0, tiled=True)  16.4 us
    ppermute x4, waiting for transfers between devices, neighbours(): before = lax.ppermute(last, 'grid', [(i, i + 1) for i in range(size - 1)])  13.9 us
    all_to_all x1, waiting for transfers between devices, local(): lax.all_to_all(packed, 'grid', split_axis=0, concat_axis=0, tiled=True)  11 us
  transfers between devices with their start and end apart: 23, of which 13 were waited for; matrix products, arithmetic and copies ran while one was open for 25% of the time, Pallas kernels for 0%

profile of v2, /device:TPU:0, one launch (start us, length us, event | category | flops | bytes accessed | tf_op | source)
XLA Modules:
  0.0 279.2 jit_solution(11282849495007592284)
XLA Ops:
  1.9 3.0 %collective-permute-start.1 = (bf16[2,1024,128]{2,1,0:T(8,128)(2,1)S(1)}, bf16[2,1024,128]{2,1,0:T(8,128)(2,1)S(1)}, u32[]{:S(2)}, u32[]{:S(2)}) collective-permute-start(bf16[2,1024,128]{2,1,0:T(8,128)(2,1)S(1)} %pad_maximum_fusion.14), channel_id=1, source_target_pairs={{0,2},{1,3},{2,0},{3,1},{4,6},{5,7},{6,4},{7,5},{8,10},{9,11},{10,... | collective-permute-start | bytes 1572872 | tf_op jit(solution)/shard_map/ppermute | solution.py:108
  5.8 11.9 %collective-permute-done.1 = bf16[2,1024,128]{2,1,0:T(8,128)(2,1)S(1)} collective-permute-done((bf16[2,1024,128]{2,1,0:T(8,128)(2,1)S(1)}, bf16[2,1024,128]{2,1,0:T(8,128)(2,1)S(1)}, u32[]{:S(2)}, u32[]{:S(2)}) %collective-permute-start.1) | collective-permute-done | bytes 524320 | tf_op jit(solution)/shard_map/ppermute | solution.py:108
  18.5 9.8 %collective-permute-done.5 = bf16[2,1024,128]{2,1,0:T(8,128)(2,1)} collective-permute-done((bf16[2,1024,128]{2,1,0:T(8,128)(2,1)S(1)}, bf16[2,1024,128]{2,1,0:T(8,128)(2,1)}, u32[]{:S(2)}, u32[]{:S(2)}) %collective-permute-start.5) | collective-permute-done | bytes 524320 | tf_op jit(solution)/shard_map/ppermute | solution.py:108
  28.3 1.9 convolution_convert_fusion.1
  30.3 3.6 %collective-permute-start.3 = (bf16[1,1024,128]{2,1,0:T(8,128)(2,1)S(1)}, bf16[1,1024,128]{2,1,0:T(8,128)(2,1)S(1)}, u32[]{:S(2)}, u32[]{:S(2)}) collective-permute-start(bf16[1,1024,128]{2,1,0:T(8,128)(2,1)S(1)} %slice.572), channel_id=1, source_target_pairs={{0,4},{4,8},{8,12},{12,16},{16,20},{20,24},{24,28},{1,5},{5,9},{9,... | collective-permute-start | bytes 786440 | tf_op jit(solution)/shard_map/ppermute | solution.py:73
  34.0 2.1 convolution_convert_fusion
  36.2 4.0 %collective-permute-done.3 = bf16[1,1024,128]{2,1,0:T(8,128)(2,1)S(1)} collective-permute-done((bf16[1,1024,128]{2,1,0:T(8,128)(2,1)S(1)}, bf16[1,1024,128]{2,1,0:T(8,128)(2,1)S(1)}, u32[]{:S(2)}, u32[]{:S(2)}) %collective-permute-start.3) | collective-permute-done | bytes 262176 | tf_op jit(solution)/shard_map/ppermute | solution.py:73
  46.0 5.7 %collective-permute-start.8 = (bf16[1,1024,128]{2,1,0:T(8,128)(2,1)S(1)}, bf16[1,1024,128]{2,1,0:T(8,128)(2,1)S(1)}, u32[]{:S(2)}, u32[]{:S(2)}) collective-permute-start(bf16[1,1024,128]{2,1,0:T(8,128)(2,1)S(1)} %get-tuple-element.106), channel_id=1, source_target_pairs={{0,4},{4,8},{8,12},{12,16},{16,20},{20,24},{24,28},{1,5},{5,9},{9,... | collective-permute-start | bytes 786440 | tf_op jit(solution)/shard_map/ppermute | solution.py:73
  51.7 3.0 %collective-permute-done.7 = bf16[1,1024,128]{2,1,0:T(8,128)(2,1)} collective-permute-done((bf16[1,1024,128]{2,1,0:T(8,128)(2,1)}, bf16[1,1024,128]{2,1,0:T(8,128)(2,1)}, u32[]{:S(2)}, u32[]{:S(2)}) %collective-permute-start.7) | collective-permute-done | bytes 262176 | tf_op jit(solution)/shard_map/ppermute | solution.py:74
  54.7 1.7 constant_dynamic-update-slice_fusion.2
  56.3 9.1 %fusion.43 = bf16[4,1024,128]{1,2,0:T(8,128)(2,1)} fusion(bf16[1024,1024,1]{1,0,2:T(8,128)(2,1)} %constant.190, f32[128]{0:T(128)S(1)} %get-tuple-element.137, f32[128]{0:T(128)S(1)} %get-tuple-element.138, f32[128]{0:T(128)} %get-tuple-element.139, f32[128]{0:T(128)} %get-tuple-element.140, f32[128]{0:T(128)} %get-tuple-element.141, ...), kind=kOutput, calls=%fused_computation.100 | convolution fusion | flops 1096286208 | bytes 6296064 | tf_op jit(solution)/shard_map/wk,rwc->rkc/dot_general | solution.py:68
  65.5 2.6 copy.57
  68.1 12.0 %all-to-all-start = ((bf16[4,1024,128]{2,0,1:T(4,128)(2,1)}), bf16[4,1024,128]{2,0,1:T(4,128)(2,1)S(1)}, u32[]{:S(2)}, u32[]{:S(2)}) async-start(bf16[4,1024,128]{2,0,1:T(4,128)(2,1)} %copy.57), calls=%async_computation | async-start | bytes 2097152 | tf_op jit(solution)/shard_map/all_to_all | solution.py:198
  81.5 3.3 %fusion.17 = bf16[4,1024,128]{2,1,0:T(8,128)(2,1)S(1)} fusion(f32[128]{0:T(128)S(1)} %get-tuple-element.146, f32[128]{0:T(128)S(1)} %get-tuple-element.147, f32[128]{0:T(128)S(1)} %get-tuple-element.148, f32[128]{0:T(128)S(1)} %get-tuple-element.149, f32[128]{0:T(128)S(1)} %get-tuple-element.150, f32[128]{0:T(128)S(1)} %get-tuple-element.151, ...), kind=kLoop, calls=%fused_computation.58 | loop fusion | flops 22020096 | bytes 4198912 | tf_op jit(solution)/shard_map/convert_element_type | solution.py:87
  84.9 2.3 fusion.44
  87.1 12.3 %all-to-all-done = bf16[4,1024,128]{2,0,1:T(4,128)(2,1)S(1)} async-done(((bf16[4,1024,128]{2,0,1:T(4,128)(2,1)}), bf16[4,1024,128]{2,0,1:T(4,128)(2,1)S(1)}, u32[]{:S(2)}, u32[]{:S(2)}) %all-to-all-start) | async-done | bytes 1048608 | tf_op jit(solution)/shard_map/all_to_all | solution.py:198
  100.4 1.8 copy.58
  102.1 2.4 copy.60
  104.6 4.4 %all-to-all-start.1 = ((bf16[4,1024,128]{2,0,1:T(4,128)(2,1)}), bf16[4,1024,128]{2,0,1:T(4,128)(2,1)}, u32[]{:S(2)}, u32[]{:S(2)}) async-start(bf16[4,1024,128]{2,0,1:T(4,128)(2,1)} %copy.60), calls=%async_computation.1 | async-start | bytes 2097152 | tf_op jit(solution)/shard_map/all_to_all | solution.py:198
  116.5 14.5 %all-to-all-done.1 = bf16[4,1024,128]{2,0,1:T(4,128)(2,1)} async-done(((bf16[4,1024,128]{2,0,1:T(4,128)(2,1)}), bf16[4,1024,128]{2,0,1:T(4,128)(2,1)}, u32[]{:S(2)}, u32[]{:S(2)}) %all-to-all-start.1) | async-done | bytes 1048608 | tf_op jit(solution)/shard_map/all_to_all | solution.py:198
  131.0 2.6 copy.61
  135.0 4.2 %all-to-all-start.2 = ((bf16[32,128,128]{2,1,0:T(8,128)(2,1)}), bf16[32,128,128]{2,1,0:T(8,128)(2,1)}, u32[]{:S(2)}, u32[]{:S(2)}) async-start(bf16[32,128,128]{2,1,0:T(8,128)(2,1)} %copy.62), calls=%async_computation.2 | async-start | bytes 2097152 | tf_op jit(solution)/shard_map/all_to_all | solution.py:201
  139.3 1.6 fusion.112
  146.5 2.0 fusion.48
  148.5 15.0 %all-to-all-done.2 = bf16[32,128,128]{2,1,0:T(8,128)(2,1)} async-done(((bf16[32,128,128]{2,1,0:T(8,128)(2,1)}), bf16[32,128,128]{2,1,0:T(8,128)(2,1)}, u32[]{:S(2)}, u32[]{:S(2)}) %all-to-all-start.2) | async-done | bytes 1048608 | tf_op jit(solution)/shard_map/all_to_all | solution.py:201
  163.4 3.8 %all-to-all-start.3 = ((bf16[32,128,128]{2,1,0:T(8,128)(2,1)}), bf16[32,128,128]{2,1,0:T(8,128)(2,1)S(1)}, u32[]{:S(2)}, u32[]{:S(2)}) async-start(bf16[32,128,128]{2,1,0:T(8,128)(2,1)} %copy.66), calls=%async_computation.3 | async-start | bytes 2097152 | tf_op jit(solution)/shard_map/all_to_all | solution.py:201
  167.2 1.7 copy.63
  170.2 3.3 %fusion.45 = bf16[4,1024,128]{2,1,0:T(8,128)(2,1)S(1)} fusion(bf16[4,1024,128]{1,2,0:T(8,128)(2,1)} %all_to_all.57, bf16[1024,1024,1]{1,0,2:T(8,128)(2,1)} %constant.190), kind=kOutput, calls=%fused_computation.102 | convolution fusion | flops 1074266112 | bytes 4194304 | tf_op jit(solution)/shard_map/wk,rkc->rwc/dot_general | solution.py:68
  173.7 5.0 %fusion.29 = (f32[128]{0:T(128)}, f32[128]{0:T(128)}, f32[128]{0:T(128)}, f32[128]{0:T(128)}, f32[128]{0:T(128)}, /*index=5*/f32[128]{0:T(128)}, f32[128]{0:T(12...) fusion(bf16[6,1024,128]{2,1,0:T(8,128)(2,1)S(1)} %copy-done.5, ...), kind=kLoop, calls=%fused_computation.70 | loop fusion | flops 26213248 | bytes 8393216 | tf_op jit(solution)/shard_map/reduce_sum | solution.py:98
  180.6 1.8 add_convert_fusion.1
  182.4 10.3 %all-to-all-done.3 = bf16[32,128,128]{2,1,0:T(8,128)(2,1)S(1)} async-done(((bf16[32,128,128]{2,1,0:T(8,128)(2,1)}), bf16[32,128,128]{2,1,0:T(8,128)(2,1)S(1)}, u32[]{:S(2)}, u32[]{:S(2)}) %all-to-all-start.3) | async-done | bytes 1048608 | tf_op jit(solution)/shard_map/all_to_all | solution.py:201
  194.0 2.9 %fusion.46 = bf16[4,1024,128]{2,1,0:T(8,128)(2,1)S(1)} fusion(bf16[4,1024,128]{1,2,0:T(8,128)(2,1)S(1)} %all_to_all.61, bf16[1024,1024,1]{1,0,2:T(8,128)(2,1)} %constant.190), kind=kOutput, calls=%fused_computation.103 | convolution fusion | flops 1074266112 | bytes 4194304 | tf_op jit(solution)/shard_map/wk,rkc->rwc/dot_general | solution.py:68
  198.1 3.2 %collective-permute-start.10 = (bf16[1,1024,128]{2,1,0:T(8,128)(2,1)}, bf16[1,1024,128]{2,1,0:T(8,128)(2,1)S(1)}, u32[]{:S(2)}, u32[]{:S(2)}) collective-permute-start(bf16[1,1024,128]{2,1,0:T(8,128)(2,1)} %get-tuple-element.94), channel_id=1, source_target_pairs={{0,4},{4,8},{8,12},{12,16},{16,20},{20,24},{24,28},{1,5},{5,9},{9,... | collective-permute-start | bytes 786440 | tf_op jit(solution)/shard_map/ppermute | solution.py:73
  204.6 5.5 %collective-permute-start.12 = (bf16[1,1024,128]{2,1,0:T(8,128)(2,1)S(1)}, bf16[1,1024,128]{2,1,0:T(8,128)(2,1)S(1)}, u32[]{:S(2)}, u32[]{:S(2)}) collective-permute-start(bf16[1,1024,128]{2,1,0:T(8,128)(2,1)S(1)} %get-tuple-element.100), channel_id=1, source_target_pairs={{0,4},{4,8},{8,12},{12,16},{16,20},{20,24},{24,28},{1,5},{5,9},{9,... | collective-permute-start | bytes 786440 | tf_op jit(solution)/shard_map/ppermute | solution.py:73
  210.1 8.2 %collective-permute-done.10 = bf16[1,1024,128]{2,1,0:T(8,128)(2,1)S(1)} collective-permute-done((bf16[1,1024,128]{2,1,0:T(8,128)(2,1)}, bf16[1,1024,128]{2,1,0:T(8,128)(2,1)S(1)}, u32[]{:S(2)}, u32[]{:S(2)}) %collective-permute-start.10) | collective-permute-done | bytes 262176 | tf_op jit(solution)/shard_map/ppermute | solution.py:73
  221.5 1.7 collective-permute-done.12
  224.8 1.6 collective-permute-start.17
  228.0 4.8 %fusion.38 = (f32[128]{0:T(128)S(1)}, f32[128]{0:T(128)S(1)}, f32[128]{0:T(128)S(1)}, f32[128]{0:T(128)S(1)}, f32[128]{0:T(128)S(1)}, /*index=5*/f32[128]{0:T(12...) fusion(bf16[4,1024,128]{2,1,0:T(8,128)(2,1)S(1)} %fusion.46, bf16[6,1024,128]{2,1,0:T(8,128)(2,1)S(1)} %copy-done.24, ...), kind=kLoop, calls=%fused_computation.79 | loop fusion | flops 22543232 | bytes 4198912 | tf_op jit(solution)/shard_map/reduce_sum | solution.py:98
  233.7 4.9 %collective-permute-done.17 = bf16[2,1024,128]{2,1,0:T(8,128)(2,1)} collective-permute-done((bf16[2,1024,128]{2,1,0:T(8,128)(2,1)}, bf16[2,1024,128]{2,1,0:T(8,128)(2,1)}, u32[]{:S(2)}, u32[]{:S(2)}) %collective-permute-start.17) | collective-permute-done | bytes 524320 | tf_op jit(solution)/shard_map/ppermute | solution.py:133
  239.8 2.0 convert_add_fusion
  242.7 1.9 convolution_bitcast_fusion.2
  244.6 1.9 fusion.50
  246.6 1.8 convolution_bitcast_fusion
  248.5 2.0 fusion.52
  250.5 1.6 collective-permute-start.16
  252.2 4.3 %concatenate.148 = bf16[8,278,128]{2,1,0:T(8,128)(2,1)} concatenate(bf16[8,64,128]{2,1,0:T(8,128)(2,1)S(1)} %bitcast.161, bf16[8,64,128]{2,1,0:T(8,128)(2,1)S(1)} %bitcast.160, bf16[8,128,128]{2,1,0:T(8,128)(2,1)S(1)} %bitcast.159, bf16[8,4,128]{2,1,0:T(4,128)(2,1)S(1)} %bitcast.170, bf16[8,18,128]{2,1,0:T(8,128)(2,1)S(1)} %broadcast_in_dim.12), dimensions={1} | concatenate | bytes 1138688 | tf_op jit(solution)/shard_map/concatenate | solution.py:276
  256.5 5.5 %all-to-all-start.4 = ((bf16[8,278,128]{2,1,0:T(8,128)(2,1)}), bf16[8,278,128]{2,1,0:T(8,128)(2,1)S(1)}, u32[]{:S(2)}, u32[]{:S(2)}) async-start(bf16[8,278,128]{2,1,0:T(8,128)(2,1)} %concatenate.148), calls=%async_computation.4 | async-start | bytes 1146880 | tf_op jit(solution)/shard_map/all_to_all | solution.py:287
  265.7 11.0 %all-to-all-done.4 = bf16[8,278,128]{2,1,0:T(8,128)(2,1)S(1)} async-done(((bf16[8,278,128]{2,1,0:T(8,128)(2,1)}), bf16[8,278,128]{2,1,0:T(8,128)(2,1)S(1)}, u32[]{:S(2)}, u32[]{:S(2)}) %all-to-all-start.4) | async-done | bytes 569376 | tf_op jit(solution)/shard_map/all_to_all | solution.py:287
  (298 shorter events, 49.6 us)
Async XLA Ops:
  0.6 110.4 %copy-start = (bf16[1024,128]{1,0:T(8,128)(2,1)S(1)}, bf16[1024,128]{1,0:T(8,128)(2,1)}, u32[]{:S(2)}) copy-start(bf16[1024,128]{1,0:T(8,128)(2,1)} %param.15) | copy-start | bytes 786436
  1.9 28.4 %copy-start.38 = (bf16[1,1024,128]{2,1,0:T(8,128)(2,1)}, bf16[1,1024,128]{2,1,0:T(8,128)(2,1)S(1)}, u32[]{:S(2)}) copy-start(bf16[1,1024,128]{2,1,0:T(8,128)(2,1)S(1)} %get-tuple-element.108) | copy-start | bytes 786436
  1.9 28.4 %copy-start.40 = (bf16[1,1024,128]{2,1,0:T(8,128)(2,1)}, bf16[1,1024,128]{2,1,0:T(8,128)(2,1)S(1)}, u32[]{:S(2)}) copy-start(bf16[1,1024,128]{2,1,0:T(8,128)(2,1)S(1)} %get-tuple-element.109) | copy-start | bytes 786436
  1.9 15.8 %collective-permute-start.1 = (bf16[2,1024,128]{2,1,0:T(8,128)(2,1)S(1)}, bf16[2,1024,128]{2,1,0:T(8,128)(2,1)S(1)}, u32[]{:S(2)}, u32[]{:S(2)}) collective-permute-start(bf16[2,1024,128]{2,1,0:T(8,128)(2,1)S(1)} %pad_maximum_fusion.14), channel_id=1, source_target_pairs={{0,2},{1,3},{2,0},{3,1},{4,6},{5,7},{6,4},{7,5},{8,10},{9,11},{10,... | collective-permute-start | bytes 1572872 | tf_op jit(solution)/shard_map/ppermute | solution.py:108
  5.0 23.3 %collective-permute-start = (bf16[2,1024,128]{2,1,0:T(8,128)(2,1)S(1)}, bf16[2,1024,128]{2,1,0:T(8,128)(2,1)}, u32[]{:S(2)}, u32[]{:S(2)}) collective-permute-start(bf16[2,1024,128]{2,1,0:T(8,128)(2,1)S(1)} %pad_maximum_fusion.14), channel_id=1, source_target_pairs={{0,1},{1,0},{2,3},{3,2},{4,5},{5,4},{6,7},{7,6},{8,9},{9,8},{10,11... | collective-permute-start | bytes 1572872 | tf_op jit(solution)/shard_map/ppermute | solution.py:113
  5.0 29.0 %copy-start.42 = (bf16[2,1024,128]{2,1,0:T(8,128)(2,1)}, bf16[2,1024,128]{2,1,0:T(8,128)(2,1)S(1)}, u32[]{:S(2)}) copy-start(bf16[2,1024,128]{2,1,0:T(8,128)(2,1)S(1)} %slice.479) | copy-start | bytes 1572868
  5.0 23.2 %collective-permute-start.5 = (bf16[2,1024,128]{2,1,0:T(8,128)(2,1)S(1)}, bf16[2,1024,128]{2,1,0:T(8,128)(2,1)}, u32[]{:S(2)}, u32[]{:S(2)}) collective-permute-start(bf16[2,1024,128]{2,1,0:T(8,128)(2,1)S(1)} %slice.479), channel_id=1, source_target_pairs={{0,2},{1,3},{2,0},{3,1},{4,6},{5,7},{6,4},{7,5},{8,10},{9,11},{10,... | collective-permute-start | bytes 1572872 | tf_op jit(solution)/shard_map/ppermute | solution.py:108
  5.2 28.8 %collective-permute-start.4 = (bf16[2,1024,128]{2,1,0:T(8,128)(2,1)S(1)}, bf16[2,1024,128]{2,1,0:T(8,128)(2,1)}, u32[]{:S(2)}, u32[]{:S(2)}) collective-permute-start(bf16[2,1024,128]{2,1,0:T(8,128)(2,1)S(1)} %slice.479), channel_id=1, source_target_pairs={{0,1},{1,0},{2,3},{3,2},{4,5},{5,4},{6,7},{7,6},{8,9},{9,8},{10,11... | collective-permute-start | bytes 1572872 | tf_op jit(solution)/shard_map/ppermute | solution.py:113
  17.7 12.5 %copy-start.91 = (bf16[2,1024,128]{2,1,0:T(8,128)(2,1)}, bf16[2,1024,128]{2,1,0:T(8,128)(2,1)S(1)}, u32[]{:S(2)}) copy-start(bf16[2,1024,128]{2,1,0:T(8,128)(2,1)S(1)} %collective-permute-done.1) | copy-start | bytes 1572868
  17.7 10.5 %collective-permute-start.2 = (bf16[2,1024,128]{2,1,0:T(8,128)(2,1)S(1)}, bf16[2,1024,128]{2,1,0:T(8,128)(2,1)S(1)}, u32[]{:S(2)}, u32[]{:S(2)}) collective-permute-start(bf16[2,1024,128]{2,1,0:T(8,128)(2,1)S(1)} %collective-permute-done.1), channel_id=1, source_target_pairs={{0,1},{1,0},{2,3},{3,2},{4,5},{5,4},{6,7},{7,6},{8,9},{9,8},{10,11... | collective-permute-start | bytes 1572872 | tf_op jit(solution)/shard_map/ppermute | solution.py:113
  17.8 16.2 %copy-start.51 = (bf16[128,256]{1,0:T(8,128)(2,1)}, bf16[128,256]{1,0:T(8,128)(2,1)S(1)}, u32[]{:S(2)}) copy-start(bf16[128,256]{1,0:T(8,128)(2,1)S(1)} %get-tuple-element.114) | copy-start | bytes 196612
  17.8 16.2 %copy-start.54 = (bf16[128,256]{1,0:T(8,128)(2,1)}, bf16[128,256]{1,0:T(8,128)(2,1)S(1)}, u32[]{:S(2)}) copy-start(bf16[128,256]{1,0:T(8,128)(2,1)S(1)} %get-tuple-element.113) | copy-start | bytes 196612
  17.8 16.2 %copy-start.56 = (bf16[128,256]{1,0:T(8,128)(2,1)}, bf16[128,256]{1,0:T(8,128)(2,1)S(1)}, u32[]{:S(2)}) copy-start(bf16[128,256]{1,0:T(8,128)(2,1)S(1)} %get-tuple-element.115) | copy-start | bytes 196612
  18.5 37.9 %copy-start.65 = (f32[128]{0:T(128)}, f32[128]{0:T(128)S(1)}, u32[]{:S(2)}) copy-start(f32[128]{0:T(128)S(1)} %get-tuple-element.136) | copy-start | bytes 1540
  18.5 37.9 %copy-start.67 = (f32[128]{0:T(128)}, f32[128]{0:T(128)S(1)}, u32[]{:S(2)}) copy-start(f32[128]{0:T(128)S(1)} %get-tuple-element.137) | copy-start | bytes 1540
  18.5 37.9 %copy-start.69 = (f32[128]{0:T(128)}, f32[128]{0:T(128)S(1)}, u32[]{:S(2)}) copy-start(f32[128]{0:T(128)S(1)} %get-tuple-element.138) | copy-start | bytes 1540
  28.2 5.7 %collective-permute-start.6 = (bf16[2,1024,128]{2,1,0:T(8,128)(2,1)}, bf16[2,1024,128]{2,1,0:T(8,128)(2,1)S(1)}, u32[]{:S(2)}, u32[]{:S(2)}) collective-permute-start(bf16[2,1024,128]{2,1,0:T(8,128)(2,1)} %collective-permute-done.5), channel_id=1, source_target_pairs={{0,1},{1,0},{2,3},{3,2},{4,5},{5,4},{6,7},{7,6},{8,9},{9,8},{10,11... | collective-permute-start | bytes 1572872 | tf_op jit(solution)/shard_map/ppermute | solution.py:113
  30.3 5.8 %copy-start.30 = (bf16[1,1024,128]{2,1,0:T(8,128)(2,1)}, bf16[1,1024,128]{2,1,0:T(8,128)(2,1)S(1)}, u32[]{:S(2)}) copy-start(bf16[1,1024,128]{2,1,0:T(8,128)(2,1)S(1)} %slice.572) | copy-start | bytes 786436
  30.3 9.8 %collective-permute-start.3 = (bf16[1,1024,128]{2,1,0:T(8,128)(2,1)S(1)}, bf16[1,1024,128]{2,1,0:T(8,128)(2,1)S(1)}, u32[]{:S(2)}, u32[]{:S(2)}) collective-permute-start(bf16[1,1024,128]{2,1,0:T(8,128)(2,1)S(1)} %slice.572), channel_id=1, source_target_pairs={{0,4},{4,8},{8,12},{12,16},{16,20},{20,24},{24,28},{1,5},{5,9},{9,... | collective-permute-start | bytes 786440 | tf_op jit(solution)/shard_map/ppermute | solution.py:73
  33.9 47.5 %copy-start.59 = (f32[128]{0:T(128)}, f32[128]{0:T(128)S(1)}, u32[]{:S(2)}) copy-start(f32[128]{0:T(128)S(1)} %get-tuple-element.153) | copy-start | bytes 1540
  40.5 25.0 %copy-start.25 = (bf16[2,1024,128]{2,1,0:T(8,128)(2,1)}, bf16[2,1024,128]{2,1,0:T(8,128)(2,1)S(1)}, u32[]{:S(2)}) copy-start(bf16[2,1024,128]{2,1,0:T(8,128)(2,1)S(1)} %get-tuple-element.103) | copy-start | bytes 1572868
  40.5 40.9 %copy-start.8 = (bf16[2,1024,128]{2,1,0:T(8,128)(2,1)}, bf16[2,1024,128]{2,1,0:T(8,128)(2,1)S(1)}, u32[]{:S(2)}) copy-start(bf16[2,1024,128]{2,1,0:T(8,128)(2,1)S(1)} %get-tuple-element.101) | copy-start | bytes 1572868
  41.6 23.8 %copy-start.17 = (bf16[1,1024,128]{2,1,0:T(8,128)(2,1)}, bf16[1,1024,128]{2,1,0:T(8,128)(2,1)S(1)}, u32[]{:S(2)}) copy-start(bf16[1,1024,128]{2,1,0:T(8,128)(2,1)S(1)} %get-tuple-element.104) | copy-start | bytes 786436
  41.6 23.8 %copy-start.20 = (bf16[1,1024,128]{2,1,0:T(8,128)(2,1)}, bf16[1,1024,128]{2,1,0:T(8,128)(2,1)S(1)}, u32[]{:S(2)}) copy-start(bf16[1,1024,128]{2,1,0:T(8,128)(2,1)S(1)} %get-tuple-element.106) | copy-start | bytes 786436
  42.8 11.8 %collective-permute-start.7 = (bf16[1,1024,128]{2,1,0:T(8,128)(2,1)}, bf16[1,1024,128]{2,1,0:T(8,128)(2,1)}, u32[]{:S(2)}, u32[]{:S(2)}) collective-permute-start(bf16[1,1024,128]{2,1,0:T(8,128)(2,1)} %get-tuple-element.107), channel_id=1, source_target_pairs={{4,0},{8,4},{12,8},{16,12},{20,16},{24,20},{28,24},{5,1},{9,5},{13... | collective-permute-start | bytes 786440 | tf_op jit(solution)/shard_map/ppermute | solution.py:74
  44.7 20.7 %collective-permute-start.9 = (bf16[1,1024,128]{2,1,0:T(8,128)(2,1)S(1)}, bf16[1,1024,128]{2,1,0:T(8,128)(2,1)S(1)}, u32[]{:S(2)}, u32[]{:S(2)}) collective-permute-start(bf16[1,1024,128]{2,1,0:T(8,128)(2,1)S(1)} %get-tuple-element.104), channel_id=1, source_target_pairs={{4,0},{8,4},{12,8},{16,12},{20,16},{24,20},{28,24},{5,1},{9,5},{13... | collective-permute-start | bytes 786440 | tf_op jit(solution)/shard_map/ppermute | solution.py:74
  46.0 19.5 %collective-permute-start.8 = (bf16[1,1024,128]{2,1,0:T(8,128)(2,1)S(1)}, bf16[1,1024,128]{2,1,0:T(8,128)(2,1)S(1)}, u32[]{:S(2)}, u32[]{:S(2)}) collective-permute-start(bf16[1,1024,128]{2,1,0:T(8,128)(2,1)S(1)} %get-tuple-element.106), channel_id=1, source_target_pairs={{0,4},{4,8},{8,12},{12,16},{16,20},{20,24},{24,28},{1,5},{5,9},{9,... | collective-permute-start | bytes 786440 | tf_op jit(solution)/shard_map/ppermute | solution.py:73
  65.5 15.9 %copy-start.12 = (bf16[1,1024,128]{2,1,0:T(8,128)(2,1)}, bf16[1,1024,128]{2,1,0:T(8,128)(2,1)S(1)}, u32[]{:S(2)}) copy-start(bf16[1,1024,128]{2,1,0:T(8,128)(2,1)S(1)} %collective-permute-done.9) | copy-start | bytes 786436
  65.5 15.9 %copy-start.14 = (bf16[1,1024,128]{2,1,0:T(8,128)(2,1)}, bf16[1,1024,128]{2,1,0:T(8,128)(2,1)S(1)}, u32[]{:S(2)}) copy-start(bf16[1,1024,128]{2,1,0:T(8,128)(2,1)S(1)} %collective-permute-done.8) | copy-start | bytes 786436
  68.1 31.3 %all-to-all-start = ((bf16[4,1024,128]{2,0,1:T(4,128)(2,1)}), bf16[4,1024,128]{2,0,1:T(4,128)(2,1)S(1)}, u32[]{:S(2)}, u32[]{:S(2)}) async-start(bf16[4,1024,128]{2,0,1:T(4,128)(2,1)} %copy.57), calls=%async_computation | async-start | bytes 2097152 | tf_op jit(solution)/shard_map/all_to_all | solution.py:198
  104.6 26.4 %all-to-all-start.1 = ((bf16[4,1024,128]{2,0,1:T(4,128)(2,1)}), bf16[4,1024,128]{2,0,1:T(4,128)(2,1)}, u32[]{:S(2)}, u32[]{:S(2)}) async-start(bf16[4,1024,128]{2,0,1:T(4,128)(2,1)} %copy.60), calls=%async_computation.1 | async-start | bytes 2097152 | tf_op jit(solution)/shard_map/all_to_all | solution.py:198
  135.0 28.4 %all-to-all-start.2 = ((bf16[32,128,128]{2,1,0:T(8,128)(2,1)}), bf16[32,128,128]{2,1,0:T(8,128)(2,1)}, u32[]{:S(2)}, u32[]{:S(2)}) async-start(bf16[32,128,128]{2,1,0:T(8,128)(2,1)} %copy.62), calls=%async_computation.2 | async-start | bytes 2097152 | tf_op jit(solution)/shard_map/all_to_all | solution.py:201
  163.4 29.2 %all-to-all-start.3 = ((bf16[32,128,128]{2,1,0:T(8,128)(2,1)}), bf16[32,128,128]{2,1,0:T(8,128)(2,1)S(1)}, u32[]{:S(2)}, u32[]{:S(2)}) async-start(bf16[32,128,128]{2,1,0:T(8,128)(2,1)} %copy.66), calls=%async_computation.3 | async-start | bytes 2097152 | tf_op jit(solution)/shard_map/all_to_all | solution.py:201
  198.0 22.1 %copy-start.44 = (bf16[2,1024,128]{2,1,0:T(8,128)(2,1)}, bf16[2,1024,128]{2,1,0:T(8,128)(2,1)S(1)}, u32[]{:S(2)}) copy-start(bf16[2,1024,128]{2,1,0:T(8,128)(2,1)S(1)} %add_convert_fusion) | copy-start | bytes 1572868
  198.1 20.1 %copy-start.29 = (bf16[2,1024,128]{2,1,0:T(8,128)(2,1)S(1)}, bf16[2,1024,128]{2,1,0:T(8,128)(2,1)}, u32[]{:S(2)}) copy-start(bf16[2,1024,128]{2,1,0:T(8,128)(2,1)} %get-tuple-element.92) | copy-start | bytes 1572868
  198.1 20.1 %collective-permute-start.10 = (bf16[1,1024,128]{2,1,0:T(8,128)(2,1)}, bf16[1,1024,128]{2,1,0:T(8,128)(2,1)S(1)}, u32[]{:S(2)}, u32[]{:S(2)}) collective-permute-start(bf16[1,1024,128]{2,1,0:T(8,128)(2,1)} %get-tuple-element.94), channel_id=1, source_target_pairs={{0,4},{4,8},{8,12},{12,16},{16,20},{20,24},{24,28},{1,5},{5,9},{9,... | collective-permute-start | bytes 786440 | tf_op jit(solution)/shard_map/ppermute | solution.py:73
  201.9 18.2 %collective-permute-start.14 = (bf16[2,1024,256]{2,1,0:T(8,128)(2,1)S(1)}, bf16[2,1024,256]{2,1,0:T(8,128)(2,1)S(1)}, u32[]{:S(2)}, u32[]{:S(2)}) collective-permute-start(bf16[2,1024,256]{2,1,0:T(8,128)(2,1)S(1)} %convolution_convert_fusion.3), channel_id=1, source_target_pairs={{0,1},{1,0},{2,3},{3,2},{4,5},{5,4},{6,7},{7,6},{8,9},{9,8},{10,11... | collective-permute-start | bytes 3145736 | tf_op jit(solution)/shard_map/ppermute | solution.py:122
  202.0 17.0 %collective-permute-start.11 = (bf16[1,1024,128]{2,1,0:T(8,128)(2,1)}, bf16[1,1024,128]{2,1,0:T(8,128)(2,1)S(1)}, u32[]{:S(2)}, u32[]{:S(2)}) collective-permute-start(bf16[1,1024,128]{2,1,0:T(8,128)(2,1)} %get-tuple-element.95), channel_id=1, source_target_pairs={{4,0},{8,4},{12,8},{16,12},{20,16},{24,20},{28,24},{5,1},{9,5},{13... | collective-permute-start | bytes 786440 | tf_op jit(solution)/shard_map/ppermute | solution.py:74
  203.3 18.2 %collective-permute-start.13 = (bf16[1,1024,128]{2,1,0:T(8,128)(2,1)S(1)}, bf16[1,1024,128]{2,1,0:T(8,128)(2,1)S(1)}, u32[]{:S(2)}, u32[]{:S(2)}) collective-permute-start(bf16[1,1024,128]{2,1,0:T(8,128)(2,1)S(1)} %get-tuple-element.99), channel_id=1, source_target_pairs={{4,0},{8,4},{12,8},{16,12},{20,16},{24,20},{28,24},{5,1},{9,5},{13... | collective-permute-start | bytes 786440 | tf_op jit(solution)/shard_map/ppermute | solution.py:74
  204.6 18.6 %collective-permute-start.12 = (bf16[1,1024,128]{2,1,0:T(8,128)(2,1)S(1)}, bf16[1,1024,128]{2,1,0:T(8,128)(2,1)S(1)}, u32[]{:S(2)}, u32[]{:S(2)}) collective-permute-start(bf16[1,1024,128]{2,1,0:T(8,128)(2,1)S(1)} %get-tuple-element.100), channel_id=1, source_target_pairs={{0,4},{4,8},{8,12},{12,16},{16,20},{20,24},{24,28},{1,5},{5,9},{9,... | collective-permute-start | bytes 786440 | tf_op jit(solution)/shard_map/ppermute | solution.py:73
  224.0 9.7 %copy-start.35 = (bf16[1,1024,128]{2,1,0:T(8,128)(2,1)}, bf16[1,1024,128]{2,1,0:T(8,128)(2,1)S(1)}, u32[]{:S(2)}) copy-start(bf16[1,1024,128]{2,1,0:T(8,128)(2,1)S(1)} %add_convert_fusion.4) | copy-start | bytes 786436
  224.8 8.9 %copy-start.36 = (bf16[1,1024,128]{2,1,0:T(8,128)(2,1)}, bf16[1,1024,128]{2,1,0:T(8,128)(2,1)S(1)}, u32[]{:S(2)}) copy-start(bf16[1,1024,128]{2,1,0:T(8,128)(2,1)S(1)} %add_convert_fusion.3) | copy-start | bytes 786436
  224.8 13.8 %collective-permute-start.17 = (bf16[2,1024,128]{2,1,0:T(8,128)(2,1)}, bf16[2,1024,128]{2,1,0:T(8,128)(2,1)}, u32[]{:S(2)}, u32[]{:S(2)}) collective-permute-start(bf16[2,1024,128]{2,1,0:T(8,128)(2,1)} %slice.779), channel_id=1, source_target_pairs={{0,2},{1,3},{2,0},{3,1},{4,6},{5,7},{6,4},{7,5},{8,10},{9,11},{10,... | collective-permute-start | bytes 1572872 | tf_op jit(solution)/shard_map/ppermute | solution.py:133
  227.9 11.9 %collective-permute-start.15 = (bf16[2,1024,256]{2,1,0:T(8,128)(2,1)}, bf16[2,1024,256]{2,1,0:T(8,128)(2,1)}, u32[]{:S(2)}, u32[]{:S(2)}) collective-permute-start(bf16[2,1024,256]{2,1,0:T(8,128)(2,1)} %convolution_convert_fusion.2), channel_id=1, source_target_pairs={{0,1},{1,0},{2,3},{3,2},{4,5},{5,4},{6,7},{7,6},{8,9},{9,8},{10,11... | collective-permute-start | bytes 3145736 | tf_op jit(solution)/shard_map/ppermute | solution.py:122
  233.6 6.2 %copy-start.53 = (bf16[128,256]{1,0:T(8,128)(2,1)S(1)}, bf16[128,256]{1,0:T(8,128)(2,1)}, u32[]{:S(2)}) copy-start(bf16[128,256]{1,0:T(8,128)(2,1)} %copy-done.51) | copy-start | bytes 196612
  250.5 12.9 %collective-permute-start.16 = (bf16[2,1024,128]{2,1,0:T(8,128)(2,1)}, bf16[2,1024,128]{2,1,0:T(8,128)(2,1)}, u32[]{:S(2)}, u32[]{:S(2)}) collective-permute-start(bf16[2,1024,128]{2,1,0:T(8,128)(2,1)} %slice.778), channel_id=1, source_target_pairs={{0,2},{1,3},{2,0},{3,1},{4,6},{5,7},{6,4},{7,5},{8,10},{9,11},{10,... | collective-permute-start | bytes 1572872 | tf_op jit(solution)/shard_map/ppermute | solution.py:133
  256.5 20.2 %all-to-all-start.4 = ((bf16[8,278,128]{2,1,0:T(8,128)(2,1)}), bf16[8,278,128]{2,1,0:T(8,128)(2,1)S(1)}, u32[]{:S(2)}, u32[]{:S(2)}) async-start(bf16[8,278,128]{2,1,0:T(8,128)(2,1)} %concatenate.148), calls=%async_computation.4 | async-start | bytes 1146880 | tf_op jit(solution)/shard_map/all_to_all | solution.py:287
  263.4 15.8 %copy-start.1 = (bf16[1024,128]{1,0:T(8,128)(2,1)S(1)}, bf16[1024,128]{1,0:T(8,128)(2,1)}, u32[]{:S(2)}) copy-start(bf16[1024,128]{1,0:T(8,128)(2,1)} %param.15) | copy-start | bytes 786436
  (72 other events, 225.8 us)
